TPU v7x, 512 devices: a whole 4x8x8 slice. The times are simulated.
512 devices in a mesh: gx: 8 (over y_lo, core), gy: 8 (over x, y_hi), gz: 8 (over z).
Axes of the slice: x: 4, y: 8 (y_hi: 2, y_lo: 4; y = y_hi * 4 + y_lo), z: 8, core: 2. Of those that a mesh axis runs over, the one named last changes fastest.
Arguments:
- particle_local_offsets: float32 [3, 16, 16, 32, 128], P(None, None, 'gx', 'gy', 'gz'), may hold values from 0 to 1, as said below
- particle_velocity: float32 [3, 16, 16, 32, 128], P(None, None, 'gx', 'gy', 'gz'), may hold values from -6 to 6
- stochastic_kicks: float32 [2, 3, 16, 16, 32, 128], P(None, None, None, 'gx', 'gy', 'gz'), may hold values from -6 to 6
- thermal_mesh_entry: int32 [16, 16, 32, 128], P(None, 'gx', 'gy', 'gz'), may hold values from 0 to 7, as said below
- occupant_tally: int32 [16, 32, 128], P('gx', 'gy', 'gz'), may hold values from 4 to 16
- fermion_thermal_level: float32 [32, 64, 256], P('gx', ('gy', 'gz')), may hold values from 0.35 to 6.3
- fluence_profile: float32 [32, 64], P('gx', ('gy', 'gz')), may hold values from 0.5 to 9
Outputs:
- new_positions: float32 [3, 16, 16, 32, 128], P(None, None, 'gx', 'gy', 'gz')
- new_velocities: float32 [3, 16, 16, 32, 128], P(None, None, 'gx', 'gy', 'gz')
- fermion_thermal_next: float32 [32, 64, 256], P('gx', ('gy', 'gz'))
Inputs may be any that keep to these rules, and one draw needn't show every extreme that they name: `particle_local_offsets`: each component of a slot's offset lies in the half of the cell that thermal_mesh_entry names for it: [b/2, (b+1)/2) with b the bit of 4 bx + 2 by + bz for that component. `thermal_mesh_entry`: 4 bx + 2 by + bz for the half along x, y and depth of the cell in which the slot's atom starts.
All inputs are finite; a program needn't handle non-finite values.
Results may differ from a plain program's by a relative error of at most 0.0003.
Values sent between devices are 32-bit elements; how exact they have to be, the bound alone decides.
A program may use at most 192 MiB of HBM per device.

v0:
```python
import jax
import jax.numpy as jnp
from jax import lax
from jax.sharding import PartitionSpec as P

SOLVER_SUBTIMES = 16


CLOCK_INCREMENT = 0.03
DRAG_RATE = 1.0
DENSITY_DECAY = 2.0
PAIR_SCALE = 1.0
PAIR_DECAY = 3.0
EMBEDDING = 10.0
SPECIFIC_WARMING = 2.0
DIFFUSION = 0.08
LASER_GAIN = 0.02
NEIGHBOUR_CELLS = [
    (along_x, along_y, along_z)
    for along_x in (-1, 0, 1)
    for along_y in (-1, 0, 1)
    for along_z in (-1, 0, 1)
]


def extended_2(block, sides, width):
    for axis, dim in sides:
        count = lax.axis_size(axis)
        forward = [(i, i + 1) for i in range(count - 1)]
        forward.append((count - 1, 0))
        backward = [(target, source) for source, target in forward]
        low = lax.ppermute(
            lax.slice_in_dim(block, block.shape[dim] - width, None, axis=dim), axis, forward
        )
        high = lax.ppermute(lax.slice_in_dim(block, 0, width, axis=dim), axis, backward)
        block = jnp.concatenate([low, block, high], axis=dim)
    return block


def pair_weights(squared):
    reach_left = jnp.maximum(1.0 - squared, 0.0)
    spread = jnp.exp(-DENSITY_DECAY * squared)
    repulse = PAIR_SCALE * jnp.exp(-PAIR_DECAY * squared)
    density = spread * reach_left * reach_left
    density_slope = spread * (-DENSITY_DECAY * reach_left * reach_left - 2.0 * reach_left)
    pair_slope = repulse * (-PAIR_DECAY * reach_left * reach_left - 2.0 * reach_left)
    return (density, density_slope, pair_slope)


def embedding_slope(density):
    return -0.5 * EMBEDDING / jnp.sqrt(1.0 + density)


def conductivity(current):
    squared = current * current
    return 1.0 + squared / (1.0 + squared)


def coupled_partitions(grid_cells):
    cells_x = grid_cells.shape[0] // 2
    cells_y = grid_cells.shape[1] // 2
    cells_z = grid_cells.shape[2] // 2
    return (
        grid_cells.reshape(cells_x, 2, cells_y, 2, cells_z, 2)
        .transpose(1, 3, 5, 0, 2, 4)
        .reshape(8, cells_x, cells_y, cells_z)
    )


def grid_of(halves):
    cells_x, cells_y, cells_z = (halves.shape[1], halves.shape[2], halves.shape[3])
    return (
        halves.reshape(2, 2, 2, cells_x, cells_y, cells_z)
        .transpose(3, 0, 4, 1, 5, 2)
        .reshape(2 * cells_x, 2 * cells_y, 2 * cells_z)
    )


def window(source, start, extent):
    leading = tuple(source.shape[:-3])
    begin = (0,) * len(leading) + tuple(start)
    finish = leading + tuple((first + length for first, length in zip(start, extent)))
    return lax.slice(source, begin, finish).reshape(leading + (-1,))


def separations(home_atoms, neighbour, delta_cell):
    offset = jnp.array(delta_cell, jnp.float32).reshape(3, 1, 1, 1)
    separation = neighbour[:3, None, :, :] + offset - home_atoms[:3, :, None, :]
    return (separation, jnp.sum(separation * separation, axis=0))


def presence(neighbour, delta_cell, slot_count):
    present = neighbour[3][None]
    if delta_cell == (0, 0, 0):
        present = present * (1.0 - jnp.eye(slot_count, dtype=jnp.float32))[:, :, None]
    return present


def pair_density(source, extent):
    slot_count = source.shape[1]
    home_atoms = window(source, (1, 1, 1), extent)
    summed = jnp.zeros(home_atoms.shape[1:], jnp.float32)
    for delta_cell in NEIGHBOUR_CELLS:
        corner = tuple((1 + delta for delta in delta_cell))
        neighbour = window(source, corner, extent)
        separation, squared = separations(home_atoms, neighbour, delta_cell)
        density = pair_weights(squared)[0]
        summed = summed + jnp.sum(density * presence(neighbour, delta_cell, slot_count), axis=1)
    return (summed * home_atoms[3]).reshape((slot_count,) + tuple(extent))


def pair_forces(source, slopes, extent):
    slot_count = source.shape[1]
    home_atoms = window(source, (1, 1, 1), extent)
    own_slope = window(slopes, (1, 1, 1), extent)
    summed = jnp.zeros((3,) + home_atoms.shape[1:], jnp.float32)
    for delta_cell in NEIGHBOUR_CELLS:
        corner = tuple((1 + delta for delta in delta_cell))
        neighbour = window(source, corner, extent)
        far_slope = window(slopes, corner, extent)
        separation, squared = separations(home_atoms, neighbour, delta_cell)
        weights = pair_weights(squared)
        strength = (
            (own_slope[:, None, :] + far_slope[None, :, :]) * weights[1] + weights[2]
        ) * presence(neighbour, delta_cell, slot_count)
        summed = summed + 2.0 * jnp.sum(strength[None] * separation, axis=2)
    return (summed * home_atoms[3][None]).reshape((3, slot_count) + tuple(extent))


def close_depth(extended, width, depth_index, depth_last):
    vertical_mesh_index = extended.shape[-1]
    layer_index = jnp.arange(vertical_mesh_index)
    outside = (layer_index < width) & (depth_index == 0) | (
        layer_index >= vertical_mesh_index - width
    ) & (depth_index == depth_last)
    keep_mask = jnp.where(outside, 0.0, 1.0).astype(jnp.float32)
    return jnp.concatenate([extended[:3], (extended[3] * keep_mask)[None]], axis=0)


def flow_along(padded, along_axis):
    conduct = conductivity(padded)
    extent_size = padded.shape[along_axis]
    low_temp = lax.slice_in_dim(padded, 0, extent_size - 1, axis=along_axis)
    high_temp = lax.slice_in_dim(padded, 1, extent_size, axis=along_axis)
    low_cond = lax.slice_in_dim(conduct, 0, extent_size - 1, axis=along_axis)
    high_cond = lax.slice_in_dim(conduct, 1, extent_size, axis=along_axis)
    face_flux = 0.5 * (low_cond + high_cond) * (high_temp - low_temp)
    return lax.slice_in_dim(face_flux, 1, extent_size - 1, axis=along_axis) - lax.slice_in_dim(
        face_flux, 0, extent_size - 2, axis=along_axis
    )


def lateral_flow(side_padded):
    return flow_along(side_padded[:, 1:-1, :], 0) + flow_along(side_padded[1:-1, :, :], 1)


def closed_depth_flow(current):
    conduct = conductivity(current)
    face_flux = (
        0.5 * (conduct[:, :, :-1] + conduct[:, :, 1:]) * (current[:, :, 1:] - current[:, :, :-1])
    )
    zero_face = jnp.zeros(face_flux.shape[:2] + (1,), jnp.float32)
    return jnp.concatenate([face_flux, zero_face], axis=2) - jnp.concatenate(
        [zero_face, face_flux], axis=2
    )


def shards(
    particle_local_offsets,
    particle_velocity,
    stochastic_kicks,
    thermal_mesh_entry,
    occupant_tally,
    fermion_thermal_level,
    fluence_profile,
):
    slot_count = particle_local_offsets.shape[1]
    tile_cells = tuple(particle_local_offsets.shape[2:])
    depth_index = lax.axis_index("gz")
    depth_last = lax.axis_size("gz") - 1
    slot_order = jnp.arange(slot_count, dtype=jnp.int32)
    occupied = (slot_order[:, None, None, None] < occupant_tally[None]).astype(jnp.float32)
    region_thermal_level = lax.all_to_all(
        fermion_thermal_level, "gz", split_axis=2, concat_axis=1, tiled=True
    )
    interior_partition = (
        thermal_mesh_entry[None] == jnp.arange(8, dtype=jnp.int32)[:, None, None, None, None]
    )
    nuclei_thermal_level = jnp.sum(
        jnp.where(interior_partition, coupled_partitions(region_thermal_level)[:, None], 0.0),
        axis=0,
    )
    handed_over = jnp.zeros(occupied.shape, jnp.float32)
    for momentum_total in range(stochastic_kicks.shape[0]):
        atom_data = jnp.concatenate([particle_local_offsets, occupied[None]], axis=0)
        extended = extended_2(atom_data, (("gx", 2), ("gy", 3), ("gz", 4)), 1)
        extended = close_depth(extended, 1, depth_index, depth_last)
        slopes = embedding_slope(pair_density(extended, tile_cells))
        slope_cycle = extended_2(slopes, (("gx", 1), ("gy", 2), ("gz", 3)), 1)
        forces = pair_forces(extended, slope_cycle, tile_cells)
        jolted_speeds = particle_velocity + CLOCK_INCREMENT * forces
        slowed_speeds = (1.0 - DRAG_RATE * CLOCK_INCREMENT) * jolted_speeds + jnp.sqrt(
            2.0 * DRAG_RATE * CLOCK_INCREMENT * nuclei_thermal_level
        )[None] * stochastic_kicks[momentum_total]
        handed_over = handed_over + occupied * 0.5 * (
            jnp.sum(jolted_speeds * jolted_speeds, axis=0)
            - jnp.sum(slowed_speeds * slowed_speeds, axis=0)
        )
        particle_velocity = (
            occupied[None] * slowed_speeds + (1.0 - occupied[None]) * particle_velocity
        )
        particle_local_offsets = particle_local_offsets + CLOCK_INCREMENT * (
            occupied[None] * slowed_speeds
        )
    deposit_tile = grid_of(jnp.sum(jnp.where(interior_partition, handed_over[None], 0.0), axis=1))
    optical_power_source = lax.all_to_all(
        deposit_tile, "gz", split_axis=1, concat_axis=2, tiled=True
    )
    excited_fermions = fermion_thermal_level + optical_power_source / SPECIFIC_WARMING
    vertical_mesh_index = fermion_thermal_level.shape[2]
    depth_decay = jnp.exp(
        -(jnp.arange(vertical_mesh_index).astype(jnp.float32) + 0.5) / (0.25 * vertical_mesh_index)
    )
    source = LASER_GAIN * fluence_profile[:, :, None] * depth_decay[None, None, :]

    def conduction_sweep(substep_index, current):
        side_padded = extended_2(current, (("gx", 0), (("gy", "gz"), 1)), 1)
        return (
            current + DIFFUSION * (lateral_flow(side_padded) + closed_depth_flow(current)) + source
        )

    fermion_thermal_next = lax.fori_loop(0, SOLVER_SUBTIMES, conduction_sweep, excited_fermions)
    return (particle_local_offsets, particle_velocity, fermion_thermal_next)


def solution(mesh):
    placed = (
        P(None, None, "gx", "gy", "gz"),
        P(None, None, "gx", "gy", "gz"),
        P(None, None, None, "gx", "gy", "gz"),
        P(None, "gx", "gy", "gz"),
        P("gx", "gy", "gz"),
        P("gx", ("gy", "gz"), None),
        P("gx", ("gy", "gz")),
    )
    return jax.shard_map(
        shards,
        mesh=mesh,
        in_specs=placed,
        out_specs=(
            P(None, None, "gx", "gy", "gz"),
            P(None, None, "gx", "gy", "gz"),
            P("gx", ("gy", "gz"), None),
        ),
        check_vma=False,
    )
```

profile of v0, /device:TPU:1, one launch (start us, length us, event | category | flops | bytes accessed | tf_op | source)
XLA Modules:
  0.0 865.2 jit_solution(11835367500827457061)
XLA Ops:
  3.8 11.0 %all-to-all-start = ((f32[8,1,128]{2,1,0:T(1,128)}), f32[8,1,128]{2,1,0:T(1,128)S(1)}, u32[]{:S(2)}, u32[]{:S(2)}) async-start(f32[8,1,128]{2,1,0:T(1,128)} %reshape.3500), calls=%async_computation | async-start | bytes 8192 | tf_op jit(solution)/shard_map/all_to_all | solution.py:183
  154.8 8.4 collective-permute-start.10
  387.2 8.1 collective-permute-start.25
  466.2 398.2 %while.11 = (s32[]{:T(128)}, f32[4,1,256]{2,1,0:T(1,128)S(1)}, f32[256]{0:T(256)S(1)}, f32[4]{0:T(128)S(1)}, s32[]{:T(128)}) while((s32[]{:T(128)}, f32[4,1,256]{2,1,0:T(1,128)S(1)}, f32[256]{0:T(256)S(1)}, f32[4]{0:T(128)S(1)}, s32[]{:T(128)}) %tuple.357), condition=%wide.region_223.224_spmd.clone, body=%wide.region_222.223_spmd.clone.sunk | while | flops 61938 | bytes 235661 | solution.py:232
  477.5 9.0 %collective-permute-start.3 = (f32[6,1,256]{2,1,0:T(1,128)S(1)}, f32[6,1,256]{2,1,0:T(1,128)S(1)}, u32[]{:S(2)}, u32[]{:S(2)}) collective-permute-start(f32[6,1,256]{2,1,0:T(1,128)S(1)} %constant_dynamic-update-slice_fusion.8), channel_id=1, source_target_pairs={{1,0},{2,1},{3,2},{4,3},{5,4},{6,5},{7,6},{8,7},{9,8},{10,9},{11,1... | collective-permute-start | bytes 18440 | tf_op jit(solution)/shard_map/while/body/eval_jaxpr/ppermute | solution.py:35
  488.5 10.5 %collective-permute-done.2 = f32[6,1,256]{2,1,0:T(1,128)S(1)} collective-permute-done((f32[6,1,256]{2,1,0:T(1,128)S(1)}, f32[6,1,256]{2,1,0:T(1,128)S(1)}, u32[]{:S(2)}, u32[]{:S(2)}) %collective-permute-start.2) | collective-permute-done | bytes 6176 | tf_op jit(solution)/shard_map/while/body/eval_jaxpr/ppermute | solution.py:32
  513.0 9.0 %collective-permute-done.2 = f32[6,1,256]{2,1,0:T(1,128)S(1)} collective-permute-done((f32[6,1,256]{2,1,0:T(1,128)S(1)}, f32[6,1,256]{2,1,0:T(1,128)S(1)}, u32[]{:S(2)}, u32[]{:S(2)}) %collective-permute-start.2) | collective-permute-done | bytes 6176 | tf_op jit(solution)/shard_map/while/body/eval_jaxpr/ppermute | solution.py:32
  537.4 9.0 %collective-permute-done.2 = f32[6,1,256]{2,1,0:T(1,128)S(1)} collective-permute-done((f32[6,1,256]{2,1,0:T(1,128)S(1)}, f32[6,1,256]{2,1,0:T(1,128)S(1)}, u32[]{:S(2)}, u32[]{:S(2)}) %collective-permute-start.2) | collective-permute-done | bytes 6176 | tf_op jit(solution)/shard_map/while/body/eval_jaxpr/ppermute | solution.py:32
  548.5 7.1 collective-permute-start.1
  561.9 9.0 %collective-permute-done.2 = f32[6,1,256]{2,1,0:T(1,128)S(1)} collective-permute-done((f32[6,1,256]{2,1,0:T(1,128)S(1)}, f32[6,1,256]{2,1,0:T(1,128)S(1)}, u32[]{:S(2)}, u32[]{:S(2)}) %collective-permute-start.2) | collective-permute-done | bytes 6176 | tf_op jit(solution)/shard_map/while/body/eval_jaxpr/ppermute | solution.py:32
  586.3 9.0 %collective-permute-done.2 = f32[6,1,256]{2,1,0:T(1,128)S(1)} collective-permute-done((f32[6,1,256]{2,1,0:T(1,128)S(1)}, f32[6,1,256]{2,1,0:T(1,128)S(1)}, u32[]{:S(2)}, u32[]{:S(2)}) %collective-permute-start.2) | collective-permute-done | bytes 6176 | tf_op jit(solution)/shard_map/while/body/eval_jaxpr/ppermute | solution.py:32
  597.4 7.1 collective-permute-start.1
  610.8 9.0 %collective-permute-done.2 = f32[6,1,256]{2,1,0:T(1,128)S(1)} collective-permute-done((f32[6,1,256]{2,1,0:T(1,128)S(1)}, f32[6,1,256]{2,1,0:T(1,128)S(1)}, u32[]{:S(2)}, u32[]{:S(2)}) %collective-permute-start.2) | collective-permute-done | bytes 6176 | tf_op jit(solution)/shard_map/while/body/eval_jaxpr/ppermute | solution.py:32
  635.2 9.0 %collective-permute-done.2 = f32[6,1,256]{2,1,0:T(1,128)S(1)} collective-permute-done((f32[6,1,256]{2,1,0:T(1,128)S(1)}, f32[6,1,256]{2,1,0:T(1,128)S(1)}, u32[]{:S(2)}, u32[]{:S(2)}) %collective-permute-start.2) | collective-permute-done | bytes 6176 | tf_op jit(solution)/shard_map/while/body/eval_jaxpr/ppermute | solution.py:32
  659.6 9.0 %collective-permute-done.2 = f32[6,1,256]{2,1,0:T(1,128)S(1)} collective-permute-done((f32[6,1,256]{2,1,0:T(1,128)S(1)}, f32[6,1,256]{2,1,0:T(1,128)S(1)}, u32[]{:S(2)}, u32[]{:S(2)}) %collective-permute-start.2) | collective-permute-done | bytes 6176 | tf_op jit(solution)/shard_map/while/body/eval_jaxpr/ppermute | solution.py:32
  684.1 9.0 %collective-permute-done.2 = f32[6,1,256]{2,1,0:T(1,128)S(1)} collective-permute-done((f32[6,1,256]{2,1,0:T(1,128)S(1)}, f32[6,1,256]{2,1,0:T(1,128)S(1)}, u32[]{:S(2)}, u32[]{:S(2)}) %collective-permute-start.2) | collective-permute-done | bytes 6176 | tf_op jit(solution)/shard_map/while/body/eval_jaxpr/ppermute | solution.py:32
  708.5 9.0 %collective-permute-done.2 = f32[6,1,256]{2,1,0:T(1,128)S(1)} collective-permute-done((f32[6,1,256]{2,1,0:T(1,128)S(1)}, f32[6,1,256]{2,1,0:T(1,128)S(1)}, u32[]{:S(2)}, u32[]{:S(2)}) %collective-permute-start.2) | collective-permute-done | bytes 6176 | tf_op jit(solution)/shard_map/while/body/eval_jaxpr/ppermute | solution.py:32
  719.7 7.1 collective-permute-start.1
  733.0 9.0 %collective-permute-done.2 = f32[6,1,256]{2,1,0:T(1,128)S(1)} collective-permute-done((f32[6,1,256]{2,1,0:T(1,128)S(1)}, f32[6,1,256]{2,1,0:T(1,128)S(1)}, u32[]{:S(2)}, u32[]{:S(2)}) %collective-permute-start.2) | collective-permute-done | bytes 6176 | tf_op jit(solution)/shard_map/while/body/eval_jaxpr/ppermute | solution.py:32
  757.4 9.0 %collective-permute-done.2 = f32[6,1,256]{2,1,0:T(1,128)S(1)} collective-permute-done((f32[6,1,256]{2,1,0:T(1,128)S(1)}, f32[6,1,256]{2,1,0:T(1,128)S(1)}, u32[]{:S(2)}, u32[]{:S(2)}) %collective-permute-start.2) | collective-permute-done | bytes 6176 | tf_op jit(solution)/shard_map/while/body/eval_jaxpr/ppermute | solution.py:32
  781.9 9.0 %collective-permute-done.2 = f32[6,1,256]{2,1,0:T(1,128)S(1)} collective-permute-done((f32[6,1,256]{2,1,0:T(1,128)S(1)}, f32[6,1,256]{2,1,0:T(1,128)S(1)}, u32[]{:S(2)}, u32[]{:S(2)}) %collective-permute-start.2) | collective-permute-done | bytes 6176 | tf_op jit(solution)/shard_map/while/body/eval_jaxpr/ppermute | solution.py:32
  806.3 9.0 %collective-permute-done.2 = f32[6,1,256]{2,1,0:T(1,128)S(1)} collective-permute-done((f32[6,1,256]{2,1,0:T(1,128)S(1)}, f32[6,1,256]{2,1,0:T(1,128)S(1)}, u32[]{:S(2)}, u32[]{:S(2)}) %collective-permute-start.2) | collective-permute-done | bytes 6176 | tf_op jit(solution)/shard_map/while/body/eval_jaxpr/ppermute | solution.py:32
  830.8 9.0 %collective-permute-done.2 = f32[6,1,256]{2,1,0:T(1,128)S(1)} collective-permute-done((f32[6,1,256]{2,1,0:T(1,128)S(1)}, f32[6,1,256]{2,1,0:T(1,128)S(1)}, u32[]{:S(2)}, u32[]{:S(2)}) %collective-permute-start.2) | collective-permute-done | bytes 6176 | tf_op jit(solution)/shard_map/while/body/eval_jaxpr/ppermute | solution.py:32
  855.2 9.0 %collective-permute-done.2 = f32[6,1,256]{2,1,0:T(1,128)S(1)} collective-permute-done((f32[6,1,256]{2,1,0:T(1,128)S(1)}, f32[6,1,256]{2,1,0:T(1,128)S(1)}, u32[]{:S(2)}, u32[]{:S(2)}) %collective-permute-start.2) | collective-permute-done | bytes 6176 | tf_op jit(solution)/shard_map/while/body/eval_jaxpr/ppermute | solution.py:32
  (1577 shorter events, 654.6 us)
Async XLA Ops:
  3.8 19.8 %all-to-all-start = ((f32[8,1,128]{2,1,0:T(1,128)}), f32[8,1,128]{2,1,0:T(1,128)S(1)}, u32[]{:S(2)}, u32[]{:S(2)}) async-start(f32[8,1,128]{2,1,0:T(1,128)} %reshape.3500), calls=%async_computation | async-start | bytes 8192 | tf_op jit(solution)/shard_map/all_to_all | solution.py:183
  46.9 16.9 %collective-permute-start.9 = (f32[4,16,4,6,1]{1,2,4,3,0:T(4,128)}, f32[4,16,4,6,1]{1,2,4,3,0:T(4,128)}, u32[]{:S(2)}, u32[]{:S(2)}) collective-permute-start(f32[4,16,4,6,1]{1,2,4,3,0:T(4,128)} %copy.208), channel_id=1, source_target_pairs={{1,0},{2,1},{3,2},{4,3},{5,4},{6,5},{7,6},{0,7},{9,8},{10,9},{11,1... | collective-permute-start | bytes 18440 | tf_op jit(solution)/shard_map/ppermute | solution.py:35
  182.9 20.6 %collective-permute-start.14 = (f32[16,4,6,1]{3,2,1,0:T(8,128)}, f32[16,4,6,1]{3,2,1,0:T(8,128)S(1)}, u32[]{:S(2)}, u32[]{:S(2)}) collective-permute-start(f32[16,4,6,1]{3,2,1,0:T(8,128)} %get-tuple-element.319), channel_id=1, source_target_pairs={{0,1},{1,2},{2,3},{3,4},{4,5},{5,6},{6,7},{7,0},{8,9},{9,10},{10,1... | collective-permute-start | bytes 4616 | tf_op jit(solution)/shard_map/ppermute | solution.py:32
  185.3 18.9 %collective-permute-start.15 = (f32[16,4,6,1]{3,2,1,0:T(8,128)}, f32[16,4,6,1]{3,2,1,0:T(8,128)}, u32[]{:S(2)}, u32[]{:S(2)}) collective-permute-start(f32[16,4,6,1]{3,2,1,0:T(8,128)} %get-tuple-element.320), channel_id=1, source_target_pairs={{1,0},{2,1},{3,2},{4,3},{5,4},{6,5},{7,6},{0,7},{9,8},{10,9},{11,1... | collective-permute-start | bytes 4616 | tf_op jit(solution)/shard_map/ppermute | solution.py:35
  252.6 13.8 %collective-permute-start.18 = (f32[4,16,4,1,16]{4,3,2,1,0:T(1,128)S(1)}, f32[4,16,4,1,16]{4,3,2,1,0:T(1,128)S(1)}, u32[]{:S(2)}, u32[]{:S(2)}) collective-permute-start(f32[4,16,4,1,16]{4,3,2,1,0:T(1,128)S(1)} %get-tuple-element.240), channel_id=1, source_target_pairs={{0,8},{8,16},{16,24},{24,32},{32,40},{40,48},{48,56},{56,0},{1,9},... | collective-permute-start | bytes 49160 | tf_op jit(solution)/shard_map/ppermute | solution.py:32
  257.7 13.3 %collective-permute-start.19 = (f32[4,16,4,1,16]{4,3,2,1,0:T(1,128)S(1)}, f32[4,16,4,1,16]{4,3,2,1,0:T(1,128)S(1)}, u32[]{:S(2)}, u32[]{:S(2)}) collective-permute-start(f32[4,16,4,1,16]{4,3,2,1,0:T(1,128)S(1)} %get-tuple-element.241), channel_id=1, source_target_pairs={{8,0},{16,8},{24,16},{32,24},{40,32},{48,40},{56,48},{0,56},{9,1},... | collective-permute-start | bytes 49160 | tf_op jit(solution)/shard_map/ppermute | solution.py:35
  274.4 17.6 %collective-permute-start.21 = (f32[4,16,4,6,1]{1,2,4,3,0:T(4,128)}, f32[4,16,4,6,1]{1,2,4,3,0:T(4,128)}, u32[]{:S(2)}, u32[]{:S(2)}) collective-permute-start(f32[4,16,4,6,1]{1,2,4,3,0:T(4,128)} %copy.220), channel_id=1, source_target_pairs={{1,0},{2,1},{3,2},{4,3},{5,4},{6,5},{7,6},{0,7},{9,8},{10,9},{11,1... | collective-permute-start | bytes 18440 | tf_op jit(solution)/shard_map/ppermute | solution.py:35
  397.3 18.1 %collective-permute-start.26 = (f32[16,4,6,1]{3,2,1,0:T(8,128)}, f32[16,4,6,1]{3,2,1,0:T(8,128)S(1)}, u32[]{:S(2)}, u32[]{:S(2)}) collective-permute-start(f32[16,4,6,1]{3,2,1,0:T(8,128)} %get-tuple-element.266), channel_id=1, source_target_pairs={{0,1},{1,2},{2,3},{3,4},{4,5},{5,6},{6,7},{7,0},{8,9},{9,10},{10,1... | collective-permute-start | bytes 4616 | tf_op jit(solution)/shard_map/ppermute | solution.py:32
  399.2 16.9 %collective-permute-start.27 = (f32[16,4,6,1]{3,2,1,0:T(8,128)}, f32[16,4,6,1]{3,2,1,0:T(8,128)}, u32[]{:S(2)}, u32[]{:S(2)}) collective-permute-start(f32[16,4,6,1]{3,2,1,0:T(8,128)} %get-tuple-element.267), channel_id=1, source_target_pairs={{1,0},{2,1},{3,2},{4,3},{5,4},{6,5},{7,6},{0,7},{9,8},{10,9},{11,1... | collective-permute-start | bytes 4616 | tf_op jit(solution)/shard_map/ppermute | solution.py:35
  486.5 12.5 %collective-permute-start.2 = (f32[6,1,256]{2,1,0:T(1,128)S(1)}, f32[6,1,256]{2,1,0:T(1,128)S(1)}, u32[]{:S(2)}, u32[]{:S(2)}) collective-permute-start(f32[6,1,256]{2,1,0:T(1,128)S(1)} %constant_dynamic-update-slice_fusion.8), channel_id=1, source_target_pairs={{0,1},{1,2},{2,3},{3,4},{4,5},{5,6},{6,7},{7,8},{8,9},{9,10},{10,1... | collective-permute-start | bytes 18440 | tf_op jit(solution)/shard_map/while/body/eval_jaxpr/ppermute | solution.py:32
  509.5 12.5 %collective-permute-start.2 = (f32[6,1,256]{2,1,0:T(1,128)S(1)}, f32[6,1,256]{2,1,0:T(1,128)S(1)}, u32[]{:S(2)}, u32[]{:S(2)}) collective-permute-start(f32[6,1,256]{2,1,0:T(1,128)S(1)} %constant_dynamic-update-slice_fusion.8), channel_id=1, source_target_pairs={{0,1},{1,2},{2,3},{3,4},{4,5},{5,6},{6,7},{7,8},{8,9},{9,10},{10,1... | collective-permute-start | bytes 18440 | tf_op jit(solution)/shard_map/while/body/eval_jaxpr/ppermute | solution.py:32
  533.9 12.5 %collective-permute-start.2 = (f32[6,1,256]{2,1,0:T(1,128)S(1)}, f32[6,1,256]{2,1,0:T(1,128)S(1)}, u32[]{:S(2)}, u32[]{:S(2)}) collective-permute-start(f32[6,1,256]{2,1,0:T(1,128)S(1)} %constant_dynamic-update-slice_fusion.8), channel_id=1, source_target_pairs={{0,1},{1,2},{2,3},{3,4},{4,5},{5,6},{6,7},{7,8},{8,9},{9,10},{10,1... | collective-permute-start | bytes 18440 | tf_op jit(solution)/shard_map/while/body/eval_jaxpr/ppermute | solution.py:32
  558.4 12.5 %collective-permute-start.2 = (f32[6,1,256]{2,1,0:T(1,128)S(1)}, f32[6,1,256]{2,1,0:T(1,128)S(1)}, u32[]{:S(2)}, u32[]{:S(2)}) collective-permute-start(f32[6,1,256]{2,1,0:T(1,128)S(1)} %constant_dynamic-update-slice_fusion.8), channel_id=1, source_target_pairs={{0,1},{1,2},{2,3},{3,4},{4,5},{5,6},{6,7},{7,8},{8,9},{9,10},{10,1... | collective-permute-start | bytes 18440 | tf_op jit(solution)/shard_map/while/body/eval_jaxpr/ppermute | solution.py:32
  582.8 12.5 %collective-permute-start.2 = (f32[6,1,256]{2,1,0:T(1,128)S(1)}, f32[6,1,256]{2,1,0:T(1,128)S(1)}, u32[]{:S(2)}, u32[]{:S(2)}) collective-permute-start(f32[6,1,256]{2,1,0:T(1,128)S(1)} %constant_dynamic-update-slice_fusion.8), channel_id=1, source_target_pairs={{0,1},{1,2},{2,3},{3,4},{4,5},{5,6},{6,7},{7,8},{8,9},{9,10},{10,1... | collective-permute-start | bytes 18440 | tf_op jit(solution)/shard_map/while/body/eval_jaxpr/ppermute | solution.py:32
  607.3 12.5 %collective-permute-start.2 = (f32[6,1,256]{2,1,0:T(1,128)S(1)}, f32[6,1,256]{2,1,0:T(1,128)S(1)}, u32[]{:S(2)}, u32[]{:S(2)}) collective-permute-start(f32[6,1,256]{2,1,0:T(1,128)S(1)} %constant_dynamic-update-slice_fusion.8), channel_id=1, source_target_pairs={{0,1},{1,2},{2,3},{3,4},{4,5},{5,6},{6,7},{7,8},{8,9},{9,10},{10,1... | collective-permute-start | bytes 18440 | tf_op jit(solution)/shard_map/while/body/eval_jaxpr/ppermute | solution.py:32
  631.7 12.5 %collective-permute-start.2 = (f32[6,1,256]{2,1,0:T(1,128)S(1)}, f32[6,1,256]{2,1,0:T(1,128)S(1)}, u32[]{:S(2)}, u32[]{:S(2)}) collective-permute-start(f32[6,1,256]{2,1,0:T(1,128)S(1)} %constant_dynamic-update-slice_fusion.8), channel_id=1, source_target_pairs={{0,1},{1,2},{2,3},{3,4},{4,5},{5,6},{6,7},{7,8},{8,9},{9,10},{10,1... | collective-permute-start | bytes 18440 | tf_op jit(solution)/shard_map/while/body/eval_jaxpr/ppermute | solution.py:32
  656.2 12.5 %collective-permute-start.2 = (f32[6,1,256]{2,1,0:T(1,128)S(1)}, f32[6,1,256]{2,1,0:T(1,128)S(1)}, u32[]{:S(2)}, u32[]{:S(2)}) collective-permute-start(f32[6,1,256]{2,1,0:T(1,128)S(1)} %constant_dynamic-update-slice_fusion.8), channel_id=1, source_target_pairs={{0,1},{1,2},{2,3},{3,4},{4,5},{5,6},{6,7},{7,8},{8,9},{9,10},{10,1... | collective-permute-start | bytes 18440 | tf_op jit(solution)/shard_map/while/body/eval_jaxpr/ppermute | solution.py:32
  680.6 12.5 %collective-permute-start.2 = (f32[6,1,256]{2,1,0:T(1,128)S(1)}, f32[6,1,256]{2,1,0:T(1,128)S(1)}, u32[]{:S(2)}, u32[]{:S(2)}) collective-permute-start(f32[6,1,256]{2,1,0:T(1,128)S(1)} %constant_dynamic-update-slice_fusion.8), channel_id=1, source_target_pairs={{0,1},{1,2},{2,3},{3,4},{4,5},{5,6},{6,7},{7,8},{8,9},{9,10},{10,1... | collective-permute-start | bytes 18440 | tf_op jit(solution)/shard_map/while/body/eval_jaxpr/ppermute | solution.py:32
  705.0 12.5 %collective-permute-start.2 = (f32[6,1,256]{2,1,0:T(1,128)S(1)}, f32[6,1,256]{2,1,0:T(1,128)S(1)}, u32[]{:S(2)}, u32[]{:S(2)}) collective-permute-start(f32[6,1,256]{2,1,0:T(1,128)S(1)} %constant_dynamic-update-slice_fusion.8), channel_id=1, source_target_pairs={{0,1},{1,2},{2,3},{3,4},{4,5},{5,6},{6,7},{7,8},{8,9},{9,10},{10,1... | collective-permute-start | bytes 18440 | tf_op jit(solution)/shard_map/while/body/eval_jaxpr/ppermute | solution.py:32
  729.5 12.5 %collective-permute-start.2 = (f32[6,1,256]{2,1,0:T(1,128)S(1)}, f32[6,1,256]{2,1,0:T(1,128)S(1)}, u32[]{:S(2)}, u32[]{:S(2)}) collective-permute-start(f32[6,1,256]{2,1,0:T(1,128)S(1)} %constant_dynamic-update-slice_fusion.8), channel_id=1, source_target_pairs={{0,1},{1,2},{2,3},{3,4},{4,5},{5,6},{6,7},{7,8},{8,9},{9,10},{10,1... | collective-permute-start | bytes 18440 | tf_op jit(solution)/shard_map/while/body/eval_jaxpr/ppermute | solution.py:32
  753.9 12.5 %collective-permute-start.2 = (f32[6,1,256]{2,1,0:T(1,128)S(1)}, f32[6,1,256]{2,1,0:T(1,128)S(1)}, u32[]{:S(2)}, u32[]{:S(2)}) collective-permute-start(f32[6,1,256]{2,1,0:T(1,128)S(1)} %constant_dynamic-update-slice_fusion.8), channel_id=1, source_target_pairs={{0,1},{1,2},{2,3},{3,4},{4,5},{5,6},{6,7},{7,8},{8,9},{9,10},{10,1... | collective-permute-start | bytes 18440 | tf_op jit(solution)/shard_map/while/body/eval_jaxpr/ppermute | solution.py:32
  778.4 12.5 %collective-permute-start.2 = (f32[6,1,256]{2,1,0:T(1,128)S(1)}, f32[6,1,256]{2,1,0:T(1,128)S(1)}, u32[]{:S(2)}, u32[]{:S(2)}) collective-permute-start(f32[6,1,256]{2,1,0:T(1,128)S(1)} %constant_dynamic-update-slice_fusion.8), channel_id=1, source_target_pairs={{0,1},{1,2},{2,3},{3,4},{4,5},{5,6},{6,7},{7,8},{8,9},{9,10},{10,1... | collective-permute-start | bytes 18440 | tf_op jit(solution)/shard_map/while/body/eval_jaxpr/ppermute | solution.py:32
  802.8 12.5 %collective-permute-start.2 = (f32[6,1,256]{2,1,0:T(1,128)S(1)}, f32[6,1,256]{2,1,0:T(1,128)S(1)}, u32[]{:S(2)}, u32[]{:S(2)}) collective-permute-start(f32[6,1,256]{2,1,0:T(1,128)S(1)} %constant_dynamic-update-slice_fusion.8), channel_id=1, source_target_pairs={{0,1},{1,2},{2,3},{3,4},{4,5},{5,6},{6,7},{7,8},{8,9},{9,10},{10,1... | collective-permute-start | bytes 18440 | tf_op jit(solution)/shard_map/while/body/eval_jaxpr/ppermute | solution.py:32
  827.3 12.5 %collective-permute-start.2 = (f32[6,1,256]{2,1,0:T(1,128)S(1)}, f32[6,1,256]{2,1,0:T(1,128)S(1)}, u32[]{:S(2)}, u32[]{:S(2)}) collective-permute-start(f32[6,1,256]{2,1,0:T(1,128)S(1)} %constant_dynamic-update-slice_fusion.8), channel_id=1, source_target_pairs={{0,1},{1,2},{2,3},{3,4},{4,5},{5,6},{6,7},{7,8},{8,9},{9,10},{10,1... | collective-permute-start | bytes 18440 | tf_op jit(solution)/shard_map/while/body/eval_jaxpr/ppermute | solution.py:32
  (483 other events, 1569.0 us)
where the time goes:
time: 881 us; the launch traced here: 865 us
  starting transfers between devices  354 us (40%)
  local copies, waits for them, and re-layouts  238 us (27%)
  waiting for transfers between devices  182 us (21%)
  other arithmetic  83.4 us (9%)
    ppermute x44, starting transfers between devices, extended_2(): lax.ppermute(lax.slice_in_dim(block, 0, width, axis=dim), axis, backward)  199 us
    ppermute x44, waiting for transfers between devices, extended_2(): lax.ppermute(lax.slice_in_dim(block, block.shape[dim] - width, None, axis...  147 us
    ppermute x44, starting transfers between devices, extended_2(): lax.ppermute(lax.slice_in_dim(block, block.shape[dim] - width, None, axis...  139 us
    mul x52, local copies, waits for them, and re-layouts, pair_density(): density * presence(neighbour, delta_cell, slot_count)  59.5 us
    unnamed x842, local copies, waits for them, and re-layouts  57.8 us
    add x52, local copies, waits for them, and re-layouts, pair_forces(): own_slope[:, None, :] + far_slope[None, :, :]  54.1 us
    ppermute x44, waiting for transfers between devices, extended_2(): lax.ppermute(lax.slice_in_dim(block, 0, width, axis=dim), axis, backward)  29.4 us
    add x50, other arithmetic, separations(): separation = neighbour[:3, None, :, :] + offset - home_atoms[:3, :, None, :]  24.1 us
  transfers between devices with their start and end apart: 90, of which 41 were waited for; matrix products, arithmetic and copies ran while one was open for 6% of the time, Pallas kernels for 0%

commit v1 on v0

v1 whole, which is shorter than its diff:
```python
import itertools

import jax
import jax.numpy as jnp
from jax import lax
from jax.experimental import pallas as pl
from jax.experimental.pallas import tpu as pltpu
from jax.sharding import PartitionSpec as P

MESH = pl.DeviceIdType.MESH
F32 = jnp.float32
STEPS = 2
HALO = 8
ROUNDS = 16 // HALO
REACH = HALO // 4
FAR = 1.0e6
CUBE = [d for d in itertools.product((-1, 0, 1), repeat=3)]
AROUND = [d for d in CUBE if d != (0, 0, 0)]
WIDE = [
    d
    for d in itertools.product(range(-REACH, REACH + 1), (-1, 0, 1), (-1, 0, 1))
    if d != (0, 0, 0)
]
FULL = 8 * 3


def parts_of(pieces):
    rows, start = {}, 0
    for d in AROUND:
        if d[2] != 0:
            count = 8
        elif d[1] != 0:
            count = 8 * ((pieces + 3) // 4)
        else:
            count = 8 * pieces
        rows[d] = (start, count)
        start += count
    return rows, start


POS_ROWS, POS_TOTAL = parts_of(6)
SLOPE_ROWS, SLOPE_TOTAL = parts_of(2)


def turn(block, shift, axis=1):
    size = block.shape[axis]
    shift = shift % size
    return block if shift == 0 else pltpu.roll(block, shift, axis)


def lanes(rows=8):
    return lax.broadcasted_iota(jnp.int32, (rows, 128), 1)


def pieces_of(block):
    return [block[8 * k : 8 * k + 8] for k in range(block.shape[0] // 8)]


def packed(pieces):
    lane = lanes()
    y, z = (lane >> 4) & 3, lane & 15
    faces = {}
    for dz in (1, -1):
        face = pieces[0]
        for k, piece in enumerate(pieces):
            moved = turn(piece, k - 15 if dz == 1 else k)
            face = moved if k == 0 else jnp.where(z == k, moved, face)
        faces["z", dz] = [face]
    for dy in (1, -1):
        blocks = []
        for first in range(0, len(pieces), 4):
            face = None
            for k, piece in enumerate(pieces[first : first + 4]):
                moved = turn(piece, 16 * k - 48 if dy == 1 else 16 * k)
                face = moved if face is None else jnp.where(y == k, moved, face)
            blocks.append(face)
        faces["y", dy] = blocks
    return faces


def face_start(table, d):
    return table[d][0], table[d][1]


def neighbours(own, landed, table, blank_low, blank_high, put):
    lane = lanes()
    x, y, z = lane >> 6, (lane >> 4) & 3, lane & 15
    count = len(own)

    def column(dx, dy, dz):
        if (dx, dy, dz) == (0, 0, 0):
            return own
        start, rows = table[dx, dy, dz]
        return pieces_of(landed[start : start + rows])

    for ex in (-1, 0, 1):

        def along_x(dy, dz):
            here = column(0, dy, dz)
            if ex == 0:
                return here
            there = column(ex, dy, dz)
            if ex == 1:
                return [turn(jnp.where(x == 0, b, a), 64) for a, b in zip(here, there)]
            return [turn(jnp.where(x == 0, a, b), 64) for a, b in zip(here, there)]

        flat = {dy: along_x(dy, 0) for dy in (-1, 0, 1)}
        deep = {(dy, dz): along_x(dy, dz)[0] for dy in (-1, 0, 1) for dz in (-1, 1)}
        for dy in (-1, 0, 1):
            if blank_low is not None:
                deep[dy, -1] = jnp.where(blank_low, FAR, deep[dy, -1])
                deep[dy, 1] = jnp.where(blank_high, FAR, deep[dy, 1])
        for ey in (-1, 0, 1):
            if ey == 0:
                level = flat[0]
                ends = {dz: deep[0, dz] for dz in (-1, 1)}
            elif ey == 1:
                level = [
                    jnp.where(y == 3, turn(flat[1][k // 4], 48 - 16 * (k % 4)), turn(flat[0][k], -16))
                    for k in range(count)
                ]
                ends = {
                    dz: jnp.where(y == 3, turn(deep[1, dz], 48), turn(deep[0, dz], -16))
                    for dz in (-1, 1)
                }
            else:
                level = [
                    jnp.where(y == 0, turn(flat[-1][k // 4], -16 * (k % 4)), turn(flat[0][k], 16))
                    for k in range(count)
                ]
                ends = {
                    dz: jnp.where(y == 0, turn(deep[-1, dz], -48), turn(deep[0, dz], 16))
                    for dz in (-1, 1)
                }
            put((ex, ey, 0), level)
            put(
                (ex, ey, 1),
                [jnp.where(z == 15, turn(ends[1], 15 - k), turn(level[k], -1)) for k in range(count)],
            )
            put(
                (ex, ey, -1),
                [jnp.where(z == 0, turn(ends[-1], -k), turn(level[k], 1)) for k in range(count)],
            )


def kernel(
    first_ref, rest_ref, heat_ref,
    moved_ref, grid_ref,
    first, rest, heat, position, velocity, shown, near, near_slope, density, force,
    pos_face, pos_land, slope_face, slope_land, level_ref, handed,
    tile_out, tile_land_a, tile_land_b, tile_out_b, ext_a, ext_b, ext_src,
    back_out, back_land, row_out, row_land,
    first_sem, heat_sem, pos_sem, slope_sem, tile_sem, back_sem, row_sem,
):
    gx, gy, gz = (lax.axis_index(a) for a in ("gx", "gy", "gz"))

    def x_place(tx):
        ring = lax.rem(tx + 1, 8)
        return lax.rem(ring, 2), (ring // 2) * 2

    def y_place(ty):
        return lax.rem(ty, 4) * 2, ty // 4

    def device(xp, yp, tz):
        return (xp[0] + yp[0], xp[1] + yp[1], tz)

    ring_place = (gy // 2) * 2 + lax.rem(gx, 2)
    tx = lax.rem(ring_place + 7, 8)
    ty = lax.rem(gy, 2) * 4 + gx // 2
    tz = gz
    xs = {d: x_place(lax.rem(tx + d + 8, 8)) for d in range(-2, 3)}
    ys = {d: y_place(lax.rem(ty + d + 8, 8)) for d in (-1, 0, 1)}
    zs = {d: lax.rem(tz + d + 8, 8) for d in (-1, 0, 1)}

    def partner(d):
        return device(xs[d[0]], ys[d[1]], zs[d[2]])

    my_x, my_y = x_place(gx), y_place(gy)

    def worker(z):
        return device(my_x, my_y, z)

    def owner(z):
        return (tx, ty, z)

    barrier = pltpu.get_barrier_semaphore()
    greeted = [worker(z) for z in range(8)] + [owner(z) for z in range(8)]
    greeted += [partner(d) for d in (WIDE if REACH > 1 else AROUND)]
    for target in greeted:
        pl.semaphore_signal(barrier, inc=1, device_id=target, device_id_type=MESH)
    pl.semaphore_wait(barrier, len(greeted))

    def send(src, dst, sems, target):
        pltpu.make_async_remote_copy(
            src_ref=src, dst_ref=dst, send_sem=sems.at[0], recv_sem=sems.at[1],
            device_id=target, device_id_type=MESH,
        ).start()

    def take(ref, sem):
        pltpu.make_async_copy(ref, ref, sem).wait()

    send(first_ref, first, first_sem.at[0], worker(gz))
    for z in range(8):
        send(heat_ref.at[z], heat.at[gz], heat_sem, worker(z))
    send(rest_ref, rest, first_sem.at[1], worker(gz))

    lane = lanes()
    row = lax.broadcasted_iota(jnp.int32, (8, 128), 0)
    slot = lax.broadcasted_iota(jnp.int32, (16, 128), 0)

    take(first, first_sem.at[0, 1])
    live = slot.astype(F32) < first[48:49, :]
    live3 = jnp.concatenate([live] * 3, axis=0)
    position[...] = first[0:48, :]
    at_bottom, at_top = tz == 0, tz == 7

    def spread(own, faces, face_ref, land, table, sems):
        at = 0
        places = {}
        for key, blocks in [(("x", 0), own)] + list(faces.items()):
            for k, block in enumerate(blocks):
                face_ref[at + 8 * k : at + 8 * k + 8, :] = block
            places[key] = (at, 8 * len(blocks))
            at += 8 * len(blocks)
        for d in AROUND:
            key = ("z", d[2]) if d[2] else ("y", d[1]) if d[1] else ("x", 0)
            start, rows = places[key]
            there = tuple(-c for c in d)
            send(
                face_ref.at[pl.ds(start, rows)], land.at[pl.ds(table[there][0], rows)],
                sems, partner(d),
            )

    handed[...] = jnp.zeros((16, 128), F32)

    def dynamics(step, carry):
        own = pieces_of(jnp.where(live3, position[...], FAR))
        for k, piece in enumerate(own):
            shown[8 * k : 8 * k + 8, :] = piece
        spread(own, packed(own), pos_face.at[step], pos_land.at[step], POS_ROWS, pos_sem.at[step])
        take(pos_land.at[step], pos_sem.at[step, 1])

        def put_position(e, pieces):
            index = CUBE.index(e)
            for k, piece in enumerate(pieces):
                near[index, 8 * k : 8 * k + 8, :] = piece + float(e[k // 2])

        landed = pos_land[step]
        neighbours(own, landed, POS_ROWS, at_bottom, at_top, put_position)

        def one_density(s, carry):
            home = [shown[pl.ds(16 * c + s, 1), :] for c in range(3)]
            total = jnp.zeros((16, 128), F32)
            for index in range(27):
                d = [near[index, 16 * c : 16 * c + 16, :] - home[c] for c in range(3)]
                q = d[0] * d[0] + d[1] * d[1] + d[2] * d[2]
                w = jnp.maximum(1.0 - q, 0.0)
                total = total + jnp.exp(-2.0 * q) * (w * w)
            density[pl.ds(s, 1), :] = jnp.sum(total, axis=0, keepdims=True)
            return carry

        lax.fori_loop(0, 16, one_density, 0)
        rho = jnp.where(live, density[...] - 1.0, 0.0)
        slope = -10.0 * lax.rsqrt(1.0 + jnp.maximum(rho, 0.0))
        density[...] = slope
        own_slope = pieces_of(slope)
        spread(
            own_slope, packed(own_slope), slope_face.at[step], slope_land.at[step], SLOPE_ROWS,
            slope_sem.at[step],
        )
        take(slope_land.at[step], slope_sem.at[step, 1])

        def put_slope(e, pieces):
            index = CUBE.index(e)
            for k, piece in enumerate(pieces):
                near_slope[index, 8 * k : 8 * k + 8, :] = piece

        neighbours(own_slope, slope_land[step], SLOPE_ROWS, None, None, put_slope)

        def one_force(s, carry):
            home = [shown[pl.ds(16 * c + s, 1), :] for c in range(3)]
            home_slope = density[pl.ds(s, 1), :]
            total = [jnp.zeros((16, 128), F32) for _ in range(3)]
            for index in range(27):
                d = [near[index, 16 * c : 16 * c + 16, :] - home[c] for c in range(3)]
                q = d[0] * d[0] + d[1] * d[1] + d[2] * d[2]
                w = jnp.maximum(1.0 - q, 0.0)
                once = jnp.exp(-q)
                both = near_slope[index] + home_slope
                strength = (w * (once * once)) * (both * (w + 1.0) + once * (3.0 * w + 2.0))
                total = [t + strength * c for t, c in zip(total, d)]
            for c in range(3):
                force[pl.ds(16 * c + s, 1), :] = jnp.sum(total[c], axis=0, keepdims=True)
            return carry

        lax.fori_loop(0, 16, one_force, 0)

        @pl.when(step == 0)
        def _():
            take(rest, first_sem.at[1, 1])
            take(heat, heat_sem.at[1])
            velocity[...] = rest[0:48, :]
            entry = rest[144:160, :]
            tile = heat[:, 0, :]
            level = jnp.zeros((16, 128), F32)
            for bx, bz in itertools.product((0, 1), repeat=2):
                spread_out = jnp.dot(
                    tile, choice(bx, bz), precision=lax.Precision.HIGHEST, preferred_element_type=F32
                )
                for by in (0, 1):
                    mine = row == 2 * ((lane >> 4) & 3) + by
                    half = jnp.sum(jnp.where(mine, spread_out, 0.0), axis=0, keepdims=True)
                    level = level + jnp.where(entry == float(4 * bx + 2 * by + bz), half, 0.0)
            level_ref[...] = jnp.sqrt(0.06 * level)

        old = velocity[...]
        kicks = rest[pl.ds(pl.multiple_of(48 + 48 * step, 16), 48), :]
        kicked = old + 0.03 * jnp.where(live3, -2.0 * force[...], 0.0)
        noise = jnp.concatenate([level_ref[...]] * 3, axis=0)
        damped = 0.97 * kicked + noise * kicks
        gain = kicked * kicked - damped * damped
        handed[...] += jnp.where(live, 0.5 * (gain[0:16] + gain[16:32] + gain[32:48]), 0.0)
        velocity[...] = jnp.where(live3, damped, old)
        position[...] += 0.03 * jnp.where(live3, damped, 0.0)
        return carry

    def choice(bx, bz):
        source = lax.broadcasted_iota(jnp.int32, (128, 128), 0)
        target = lax.broadcasted_iota(jnp.int32, (128, 128), 1)
        wanted = (2 * (target >> 6) + bx) * 32 + 2 * (target & 15) + bz
        return jnp.where(source == wanted, 1.0, 0.0).astype(F32)

    lax.fori_loop(0, STEPS, dynamics, 0)

    back_out[0:48, :] = position[...]
    back_out[48:96, :] = velocity[...]
    send(back_out, back_land, back_sem, owner(tz))

    deposit = jnp.zeros((8, 128), F32)
    entry = rest[144:160, :]
    for bx, bz in itertools.product((0, 1), repeat=2):
        low, high = (
            jnp.sum(
                jnp.where(entry == float(4 * bx + 2 * by + bz), handed[...], 0.0), axis=0, keepdims=True
            )
            for by in (0, 1)
        )
        rows_y = jnp.where((row & 1) == 1, high, low)
        placed = jnp.where((row >> 1) == ((lane >> 4) & 3), rows_y, 0.0)
        deposit = deposit + lax.dot_general(
            placed, choice(bx, bz), (((1,), (1,)), ((), ())),
            precision=lax.Precision.HIGHEST, preferred_element_type=F32,
        )
    tile_out[0:8, :] = heat[:, 0, :] + 0.5 * deposit
    tile_out[8:16, :] = heat[:, 1, :]

    width = 4 + 2 * HALO
    part = lane >> 5
    depth = lax.broadcasted_iota(jnp.int32, (24, 128), 1) + (32 * tz - 32)
    inner_face = (depth >= 0) & (depth < 255)

    def extend(tile_of, ext):
        for xx in range(width):
            xt, xi = (xx - HALO) // 4, (xx - HALO) % 4
            for yt in (-1, 0, 1):
                low, mid, high = (
                    turn(tile_of((xt, yt, zt)), 32 * (zt + 1) - 32 * xi) for zt in (-1, 0, 1)
                )
                ext[xx, 8 * yt + 8 : 8 * yt + 16, :] = jnp.where(
                    part == 0, low, jnp.where(part == 1, mid, high)
                )

    def sweep(src, dst):
        def conduct(t):
            return 2.0 - 1.0 / (1.0 + t * t)

        here = src[0]
        k_here = conduct(here)
        before = None
        for xx in range(width):
            after = None
            if xx < width - 1:
                ahead = src[xx + 1]
                k_ahead = conduct(ahead)
                after = (k_here + k_ahead) * (ahead - here)
            if 0 < xx < width - 1:
                up_y = (k_here + turn(k_here, -1, 0)) * (turn(here, -1, 0) - here)
                up_z = (k_here + turn(k_here, -1)) * (turn(here, -1) - here)
                up_z = jnp.where(inner_face, up_z, 0.0)
                net = (after - before) + (up_y - turn(up_y, 1, 0)) + (up_z - turn(up_z, 1))
                dst[xx] = here + 0.04 * net + ext_src[xx]
            before = after
            if xx < width - 1:
                here, k_here = ahead, k_ahead

    def centre(ext):
        tile = None
        for xi in range(4):
            moved = turn(ext[HALO + xi, 8:16, :], 32 * xi - 32)
            tile = moved if tile is None else jnp.where(part == xi, moved, tile)
        return tile

    for turn_of in range(ROUNDS):
        out = tile_out if turn_of == 0 else tile_out_b.at[turn_of - 1]
        land = tile_land_a if turn_of == 0 else tile_land_b.at[turn_of - 1]
        if turn_of:
            out[...] = centre(ext_a)
        for index, d in enumerate(WIDE):
            there = WIDE.index(tuple(-c for c in d))
            send(out, land.at[there], tile_sem.at[turn_of], partner(d))
        take(land, tile_sem.at[turn_of, 1])
        extend(lambda d: out[0:8, :] if d == (0, 0, 0) else land[WIDE.index(d), 0:8, :], ext_a)
        if turn_of == 0:
            extend(
                lambda d: out[8:16, :] if d == (0, 0, 0) else land[WIDE.index(d), 8:16, :], ext_src
            )
            for edge in (0, width - 1):
                ext_b[edge] = ext_a[edge]

        def two(i, carry):
            sweep(ext_a, ext_b)
            sweep(ext_b, ext_a)
            return carry

        lax.fori_loop(0, HALO // 2, two, 0)

    result = centre(ext_a)
    for y in range(8):
        row_out[y, :, :] = result[y : y + 1]
        send(row_out.at[y], row_land.at[tz], row_sem, owner(y))

    take(back_land, back_sem.at[1])
    moved_ref[...] = back_land[...]
    take(row_land, row_sem.at[1])
    grid_ref[...] = row_land[...]

    take(first_ref, first_sem.at[0, 0])
    take(rest_ref, first_sem.at[1, 0])
    take(heat_ref, heat_sem.at[0])
    for step in range(STEPS):
        take(pos_land.at[step], pos_sem.at[step, 0])
        take(slope_land.at[step], slope_sem.at[step, 0])
    take(tile_land_a, tile_sem.at[0, 0])
    for turn_of in range(1, ROUNDS):
        take(tile_land_b.at[turn_of - 1], tile_sem.at[turn_of, 0])
    take(back_out, back_sem.at[0])
    take(row_out, row_sem.at[0])


def face_rows(pieces):
    return 8 * (pieces + 2 + 2 * ((pieces + 3) // 4))


def shards(
    particle_local_offsets,
    particle_velocity,
    stochastic_kicks,
    thermal_mesh_entry,
    occupant_tally,
    fermion_thermal_level,
    fluence_profile,
):
    first = jnp.concatenate(
        [
            particle_local_offsets.reshape(48, 128),
            jnp.broadcast_to(occupant_tally.astype(F32).reshape(1, 128), (8, 128)),
        ]
    )
    rest = jnp.concatenate(
        [
            particle_velocity.reshape(48, 128),
            stochastic_kicks.reshape(96, 128),
            thermal_mesh_entry.astype(F32).reshape(16, 128),
        ]
    )
    depth = fermion_thermal_level.shape[2]
    decay = jnp.exp(-(jnp.arange(depth).astype(F32) + 0.5) / (0.25 * depth))
    source = 0.02 * fluence_profile[:, :, None] * decay[None, None, :]
    heat = jnp.stack([fermion_thermal_level[:, 0], source[:, 0]], axis=0)
    heat = heat.reshape(2, 4, 8, 32).transpose(2, 0, 1, 3).reshape(8, 2, 128)

    width = 4 + 2 * HALO
    vmem = pl.BlockSpec(memory_space=pltpu.VMEM)
    buffers = [
        (56, 128), (160, 128), (8, 2, 128), (48, 128), (48, 128), (48, 128),
        (27, 48, 128), (27, 16, 128), (16, 128), (48, 128),
        (STEPS, face_rows(6), 128), (STEPS, POS_TOTAL, 128),
        (STEPS, face_rows(2), 128), (STEPS, SLOPE_TOTAL, 128),
        (16, 128), (16, 128),
        (16, 128), (len(WIDE), 16, 128), (ROUNDS - 1, len(WIDE), 8, 128), (ROUNDS - 1, 8, 128),
        (width, 24, 128), (width, 24, 128), (width, 24, 128),
        (96, 128), (96, 128), (8, 1, 128), (8, 1, 128),
    ]
    sems = [(2, 2), (2,), (STEPS, 2), (STEPS, 2), (ROUNDS, 2), (2,), (2,)]
    moved, grid = pl.pallas_call(
        kernel,
        out_shape=(
            jax.ShapeDtypeStruct((96, 128), F32),
            jax.ShapeDtypeStruct((8, 1, 128), F32),
        ),
        in_specs=[vmem] * 3,
        out_specs=(vmem, vmem),
        scratch_shapes=[pltpu.VMEM(shape, F32) for shape in buffers]
        + [pltpu.SemaphoreType.DMA(shape) for shape in sems],
        compiler_params=pltpu.CompilerParams(
            collective_id=0, has_side_effects=True, vmem_limit_bytes=32 * 1024 * 1024
        ),
    )(first, rest, heat)
    shape = particle_local_offsets.shape
    grid = grid.reshape(8, 4, 32).transpose(1, 0, 2).reshape(4, 1, 256)
    return moved[:48].reshape(shape), moved[48:].reshape(shape), grid


def solution(mesh):
    placed = (
        P(None, None, "gx", "gy", "gz"),
        P(None, None, "gx", "gy", "gz"),
        P(None, None, None, "gx", "gy", "gz"),
        P(None, "gx", "gy", "gz"),
        P("gx", "gy", "gz"),
        P("gx", ("gy", "gz"), None),
        P("gx", ("gy", "gz")),
    )
    return jax.shard_map(
        shards,
        mesh=mesh,
        in_specs=placed,
        out_specs=(
            P(None, None, "gx", "gy", "gz"),
            P(None, None, "gx", "gy", "gz"),
            P("gx", ("gy", "gz"), None),
        ),
        check_vma=False,
    )
```

time: 881 us -> 103 us (0.12)
  the two profiles are of different devices: /device:TPU:1 before, /device:TPU:5 now
where the time goes in v1:
time: 103 us
  Pallas kernels  92.7 us (90%)
  local copies, waits for them, and re-layouts  6.38 us (6%)
  other arithmetic  2.88 us (3%)
    pallas_call x1, Pallas kernels, shards(): pl.pallas_call(kernel, out_shape=(jax.ShapeDtypeStruct((96, 128), F32), j...  92.7 us

profile of v1, /device:TPU:5, one launch (start us, length us, event | category | flops | bytes accessed | tf_op | source)
XLA Modules:
  0.0 102.7 jit_solution(437141435217231884)
XLA Ops:
  0.6 0.0 copy-start
  0.6 0.7 multiply_bitcast_fusion
  1.3 0.7 convert_element_type.13
  2.0 0.1 broadcast_in_dim.4
  2.1 0.7 reduce
  2.9 0.1 broadcast_multiply_fusion
  2.9 0.1 stack.5
  3.0 0.1 reshape.82.heat_ref
  3.1 1.1 %reshape.78 = f32[48,128]{1,0:T(8,128)S(1)} reshape(f32[3,16,2,4,16]{4,3,2,1,0:T(4,128)} %param.7) | data formatting | bytes 49152 | tf_op jit(solution)/shard_map/reshape | solution.py:465
  4.2 1.1 %reshape.79 = f32[48,128]{1,0:T(8,128)S(1)} reshape(f32[3,16,2,4,16]{4,3,2,1,0:T(4,128)} %param.8) | data formatting | bytes 49152 | tf_op jit(solution)/shard_map/reshape | solution.py:471
  5.3 0.0 copy-done
  5.3 0.0 copy-start.1
  5.3 0.3 reshape.80
  5.6 0.6 copy-done.1
  6.2 0.1 reshape.81
  6.3 92.7 %shard_map.94 = (f32[96,128]{1,0:T(8,128)S(1)}, f32[8,1,128]{2,1,0:T(1,128)S(1)}) custom-call(f32[56,128]{1,0:T(8,128)S(1)} %pad_maximum_fusion.1.first_ref, f32[160,128]{1,0:T(8,128)S(1)} %pad_maximum_fusion.rest_ref, f32[8,2,128]{2,1,0:T(2,128)S(1)} %reshape.82.heat_ref), custom_call_target="tpu_custom_call" | custom-call | tf_op jit(solution)/shard_map/pallas_call | solution.py:495
  99.0 0.5 broadcast.47
  99.5 0.7 reduce.4
  100.2 0.1 reshape.85
  100.3 0.7 reshape.86
  101.0 0.9 reshape.84
  101.8 0.9 reshape.83
  (9 shorter events, 0.1 us)
Async XLA Ops:
  0.6 4.7 %copy-start = (f32[2,3,16,2,4,16]{5,4,3,2,1,0:T(4,128)S(1)}, f32[2,3,16,2,4,16]{5,4,3,2,1,0:T(4,128)}, u32[]{:S(2)}) copy-start(f32[2,3,16,2,4,16]{5,4,3,2,1,0:T(4,128)} %param.9) | copy-start | bytes 147460
  5.3 0.8 copy-start.1

commit v2 on v1

v2 whole, which is shorter than its diff:
```python
import itertools

import jax
import jax.numpy as jnp
from jax import lax
from jax.experimental import pallas as pl
from jax.experimental.pallas import tpu as pltpu
from jax.sharding import PartitionSpec as P

MESH = pl.DeviceIdType.MESH
F32 = jnp.float32
STEPS = 2
HALO = 8
ROUNDS = 16 // HALO
REACH = HALO // 4
FAR = 1.0e6
CUBE = [d for d in itertools.product((-1, 0, 1), repeat=3)]
AROUND = sorted((d for d in CUBE if d != (0, 0, 0)), key=lambda d: -sum(map(abs, d)))
WIDE = sorted(
    (
        d
        for d in itertools.product(range(-REACH, REACH + 1), (-1, 0, 1), (-1, 0, 1))
        if d != (0, 0, 0)
    ),
    key=lambda d: -sum(map(abs, d)),
)
FOLD = (4 + 2 * HALO) // 2
FLAT = [d for d in WIDE if d[2] == 0]


def parts_of(pieces):
    rows, start = {}, 0
    for d in AROUND:
        if d[2] != 0:
            count = 8
        elif d[1] != 0:
            count = 8 * ((pieces + 3) // 4)
        else:
            count = 8 * pieces
        rows[d] = (start, count)
        start += count
    return rows, start


POS_ROWS, POS_TOTAL = parts_of(6)
SLOPE_ROWS, SLOPE_TOTAL = parts_of(2)


def turn(block, shift, axis=1):
    size = block.shape[axis]
    shift = shift % size
    return block if shift == 0 else pltpu.roll(block, shift, axis)


def lanes(rows=8):
    return lax.broadcasted_iota(jnp.int32, (rows, 128), 1)


def pieces_of(block):
    return [block[8 * k : 8 * k + 8] for k in range(block.shape[0] // 8)]


def packed(pieces):
    lane = lanes()
    y, z = (lane >> 4) & 3, lane & 15
    faces = {}
    for dz in (1, -1):
        face = pieces[0]
        for k, piece in enumerate(pieces):
            moved = turn(piece, k - 15 if dz == 1 else k)
            face = moved if k == 0 else jnp.where(z == k, moved, face)
        faces["z", dz] = [face]
    for dy in (1, -1):
        blocks = []
        for first in range(0, len(pieces), 4):
            face = None
            for k, piece in enumerate(pieces[first : first + 4]):
                moved = turn(piece, 16 * k - 48 if dy == 1 else 16 * k)
                face = moved if face is None else jnp.where(y == k, moved, face)
            blocks.append(face)
        faces["y", dy] = blocks
    return faces


def face_start(table, d):
    return table[d][0], table[d][1]


def neighbours(own, landed, table, blank_low, blank_high, put):
    lane = lanes()
    x, y, z = lane >> 6, (lane >> 4) & 3, lane & 15
    count = len(own)

    def column(dx, dy, dz):
        if (dx, dy, dz) == (0, 0, 0):
            return own
        start, rows = table[dx, dy, dz]
        return pieces_of(landed[start : start + rows])

    for ex in (-1, 0, 1):

        def along_x(dy, dz):
            here = column(0, dy, dz)
            if ex == 0:
                return here
            there = column(ex, dy, dz)
            if ex == 1:
                return [turn(jnp.where(x == 0, b, a), 64) for a, b in zip(here, there)]
            return [turn(jnp.where(x == 0, a, b), 64) for a, b in zip(here, there)]

        flat = {dy: along_x(dy, 0) for dy in (-1, 0, 1)}
        deep = {(dy, dz): along_x(dy, dz)[0] for dy in (-1, 0, 1) for dz in (-1, 1)}
        for dy in (-1, 0, 1):
            if blank_low is not None:
                deep[dy, -1] = jnp.where(blank_low, FAR, deep[dy, -1])
                deep[dy, 1] = jnp.where(blank_high, FAR, deep[dy, 1])
        for ey in (-1, 0, 1):
            if ey == 0:
                level = flat[0]
                ends = {dz: deep[0, dz] for dz in (-1, 1)}
            elif ey == 1:
                level = [
                    jnp.where(y == 3, turn(flat[1][k // 4], 48 - 16 * (k % 4)), turn(flat[0][k], -16))
                    for k in range(count)
                ]
                ends = {
                    dz: jnp.where(y == 3, turn(deep[1, dz], 48), turn(deep[0, dz], -16))
                    for dz in (-1, 1)
                }
            else:
                level = [
                    jnp.where(y == 0, turn(flat[-1][k // 4], -16 * (k % 4)), turn(flat[0][k], 16))
                    for k in range(count)
                ]
                ends = {
                    dz: jnp.where(y == 0, turn(deep[-1, dz], -48), turn(deep[0, dz], 16))
                    for dz in (-1, 1)
                }
            put((ex, ey, 0), level)
            put(
                (ex, ey, 1),
                [jnp.where(z == 15, turn(ends[1], 15 - k), turn(level[k], -1)) for k in range(count)],
            )
            put(
                (ex, ey, -1),
                [jnp.where(z == 0, turn(ends[-1], -k), turn(level[k], 1)) for k in range(count)],
            )


def kernel(
    position_ref, velocity_ref, kicks_ref, entry_ref, tally_ref, level_in, fluence_ref,
    position_out, velocity_out, level_out,
    first_ref, rest_ref, heat_ref,
    first, rest, heat, position, velocity, shown, near, near_slope, near_turned, density, force,
    affinity, pos_face, pos_land, slope_face, slope_land, level_ref, handed, choice,
    tile_out, tile_land, laser_out, laser_land, ext, ext_src,
    back_out, back_land, row_out, row_land,
    first_sem, heat_sem, pos_sem, slope_sem, tile_sem, laser_sem, back_sem, row_sem,
):
    gx, gy, gz = (lax.axis_index(a) for a in ("gx", "gy", "gz"))

    def x_place(tx):
        ring = lax.rem(tx + 1, 8)
        return lax.rem(ring, 2), (ring // 2) * 2

    def y_place(ty):
        return lax.rem(ty, 4) * 2, ty // 4

    def device(xp, yp, tz):
        return (xp[0] + yp[0], xp[1] + yp[1], tz)

    ring_place = (gy // 2) * 2 + lax.rem(gx, 2)
    tx = lax.rem(ring_place + 7, 8)
    ty = lax.rem(gy, 2) * 4 + gx // 2
    tz = gz
    xs = {d: x_place(lax.rem(tx + d + 8, 8)) for d in range(-2, 3)}
    ys = {d: y_place(lax.rem(ty + d + 8, 8)) for d in (-1, 0, 1)}
    zs = {d: lax.rem(tz + d + 8, 8) for d in (-1, 0, 1)}

    def partner(d):
        return device(xs[d[0]], ys[d[1]], zs[d[2]])

    my_x, my_y = x_place(gx), y_place(gy)

    def worker(z):
        return device(my_x, my_y, z)

    def owner(z):
        return (tx, ty, z)

    barrier = pltpu.get_barrier_semaphore()
    greeted = [worker(z) for z in range(8)] + [owner(z) for z in range(8)]
    greeted += [partner(d) for d in (WIDE if REACH > 1 else AROUND)]
    for target in greeted:
        pl.semaphore_signal(barrier, inc=1, device_id=target, device_id_type=MESH)

    lane = lanes()
    row = lax.broadcasted_iota(jnp.int32, (8, 128), 0)
    slot = lax.broadcasted_iota(jnp.int32, (16, 128), 0)

    def by_lane(ref, base):
        return jnp.concatenate([ref[pl.ds(base + k, 16, stride=8), :] for k in range(8)], axis=1)

    for c in range(3):
        first_ref[16 * c : 16 * c + 16, :] = by_lane(position_ref, 128 * c)
    tally = jnp.concatenate([tally_ref[k // 4, k % 4 : k % 4 + 1, :] for k in range(8)], axis=1)
    first_ref[48:56, :] = jnp.broadcast_to(tally.astype(F32), (8, 128))
    warm, fluence = jnp.zeros((8, 128), F32), jnp.zeros((8, 128), F32)
    for x in range(4):
        upper = jnp.broadcast_to(level_in[x, :, 0:128], (8, 128))
        lower = jnp.broadcast_to(level_in[x, :, 128:256], (8, 128))
        both = jnp.where(row < 4, upper, lower)
        for k in range(4):
            warm = jnp.where(((row & 3) == k) & ((lane >> 5) == x), turn(both, 32 * x - 32 * k), warm)
        fluence = jnp.where((lane >> 5) == x, fluence_ref[0:1, x : x + 1], fluence)
    heat_ref[:, 0, :] = warm
    heat_ref[:, 1, :] = fluence

    pl.semaphore_wait(barrier, len(greeted))

    def send(src, dst, sems, target):
        pltpu.make_async_remote_copy(
            src_ref=src, dst_ref=dst, send_sem=sems.at[0], recv_sem=sems.at[1],
            device_id=target, device_id_type=MESH,
        ).start()

    def take(ref, sem):
        pltpu.make_async_copy(ref, ref, sem).wait()

    send(first_ref, first, first_sem.at[0], worker(gz))
    for z in range(8):
        send(heat_ref.at[z], heat.at[gz], heat_sem, worker(z))
    for c in range(3):
        rest_ref[16 * c : 16 * c + 16, :] = by_lane(velocity_ref, 128 * c)
    for c in range(6):
        rest_ref[48 + 16 * c : 64 + 16 * c, :] = by_lane(kicks_ref, 128 * c)
    rest_ref[144:160, :] = by_lane(entry_ref, 0).astype(F32)
    send(rest_ref, rest, first_sem.at[1], worker(gz))

    target = lax.broadcasted_iota(jnp.int32, (128, 128), 0)
    source = lax.broadcasted_iota(jnp.int32, (128, 128), 1)
    for k in range(4):
        wanted = (2 * (target >> 6) + k // 2) * 32 + 2 * (target & 15) + k % 2
        choice[128 * k : 128 * k + 128, :] = jnp.where(source == wanted, 1.0, 0.0).astype(F32)

    take(first, first_sem.at[0, 1])
    live = slot.astype(F32) < first[48:49, :]
    live3 = jnp.concatenate([live] * 3, axis=0)
    position[...] = first[0:48, :]
    at_bottom, at_top = tz == 0, tz == 7

    def spread(own, faces, face_ref, land, table, sems):
        at = 0
        places = {}
        for key, blocks in [(("x", 0), own)] + list(faces.items()):
            for k, block in enumerate(blocks):
                face_ref[at + 8 * k : at + 8 * k + 8, :] = block
            places[key] = (at, 8 * len(blocks))
            at += 8 * len(blocks)
        for d in AROUND:
            key = ("z", d[2]) if d[2] else ("y", d[1]) if d[1] else ("x", 0)
            start, rows = places[key]
            there = tuple(-c for c in d)
            send(
                face_ref.at[pl.ds(start, rows)], land.at[pl.ds(table[there][0], rows)],
                sems, partner(d),
            )

    handed[...] = jnp.zeros((16, 128), F32)

    def dynamics(step, carry):
        own = pieces_of(jnp.where(live3, position[...], FAR))
        for k, piece in enumerate(own):
            shown[8 * k : 8 * k + 8, :] = piece
        spread(own, packed(own), pos_face.at[step], pos_land.at[step], POS_ROWS, pos_sem.at[step])
        take(pos_land.at[step], pos_sem.at[step, 1])

        def put_position(e, pieces):
            index = CUBE.index(e)
            for k, piece in enumerate(pieces):
                near[index, 8 * k : 8 * k + 8, :] = piece + float(e[k // 2])

        landed = pos_land[step]
        neighbours(own, landed, POS_ROWS, at_bottom, at_top, put_position)

        def two_densities(i, carry):
            homes = [[shown[pl.ds(16 * c + 2 * i + j, 1), :] for c in range(3)] for j in (0, 1)]
            totals = [jnp.zeros((16, 128), F32) for _ in (0, 1)]
            for index in range(27):
                there = [near[index, 16 * c : 16 * c + 16, :] for c in range(3)]
                for j in (0, 1):
                    d = [there[c] - homes[j][c] for c in range(3)]
                    q = d[0] * d[0] + d[1] * d[1] + d[2] * d[2]
                    w = jnp.maximum(1.0 - q, 0.0)
                    totals[j] = totals[j] + jnp.exp(-2.0 * q) * (w * w)
            for j in (0, 1):
                density[pl.ds(2 * i + j, 1), :] = jnp.sum(totals[j], axis=0, keepdims=True)
            return carry

        lax.fori_loop(0, 8, two_densities, 0)
        rho = jnp.where(live, density[...] - 1.0, 0.0)
        slope = -10.0 * lax.rsqrt(1.0 + jnp.maximum(rho, 0.0))
        density[...] = slope
        own_slope = pieces_of(slope)
        spread(
            own_slope, packed(own_slope), slope_face.at[step], slope_land.at[step], SLOPE_ROWS,
            slope_sem.at[step],
        )

        def two_geometries(i, carry):
            homes = [[shown[pl.ds(16 * c + 2 * i + j, 1), :] for c in range(3)] for j in (0, 1)]
            home_slopes = [density[pl.ds(2 * i + j, 1), :] for j in (0, 1)]
            totals = [[jnp.zeros((16, 128), F32) for _ in range(3)] for _ in (0, 1)]
            for index in range(27):
                there = [near[index, 16 * c : 16 * c + 16, :] for c in range(3)]
                for j in (0, 1):
                    d = [there[c] - homes[j][c] for c in range(3)]
                    q = d[0] * d[0] + d[1] * d[1] + d[2] * d[2]
                    w = jnp.maximum(1.0 - q, 0.0)
                    once = jnp.exp(-q)
                    common = w * (once * once)
                    embed = common * (w + 1.0)
                    affinity[2 * i + j, index] = embed
                    strength = embed * home_slopes[j] + common * once * (3.0 * w + 2.0)
                    totals[j] = [t + strength * c for t, c in zip(totals[j], d)]
            for j in (0, 1):
                for c in range(3):
                    force[pl.ds(16 * c + 2 * i + j, 1), :] = jnp.sum(
                        totals[j][c], axis=0, keepdims=True
                    )
            return carry

        lax.fori_loop(0, 8, two_geometries, 0)

        @pl.when(step == 0)
        def _():
            take(rest, first_sem.at[1, 1])
            take(heat, heat_sem.at[1])
            velocity[...] = rest[0:48, :]
            entry = rest[144:160, :]
            spread_out = lax.dot_general(
                heat[:, 0, :], choice[...], (((1,), (1,)), ((), ())),
                precision=lax.Precision.HIGHEST, preferred_element_type=F32,
            )
            level = jnp.zeros((16, 128), F32)
            for bx, bz, by in itertools.product((0, 1), repeat=3):
                k = 2 * bx + bz
                mine = row == 2 * ((lane >> 4) & 3) + by
                half = jnp.sum(
                    jnp.where(mine, spread_out[:, 128 * k : 128 * k + 128], 0.0), axis=0, keepdims=True
                )
                level = level + jnp.where(entry == float(4 * bx + 2 * by + bz), half, 0.0)
            level_ref[...] = jnp.sqrt(0.06 * level)
            laser_out[...] = heat[:, 1, :]
            for index, d in enumerate(FLAT):
                there = FLAT.index(tuple(-c for c in d))
                send(laser_out, laser_land.at[there], laser_sem, partner(d))

        take(slope_land.at[step], slope_sem.at[step, 1])

        def put_slope(e, pieces):
            index = CUBE.index(e)
            for k, piece in enumerate(pieces):
                near_slope[index, 8 * k : 8 * k + 8, :] = piece
                for c in range(3):
                    at = 16 * c + 8 * k
                    near_turned[index, at : at + 8, :] = piece * near[index, at : at + 8, :]

        neighbours(own_slope, slope_land[step], SLOPE_ROWS, None, None, put_slope)

        def two_forces(i, carry):
            plain = [jnp.zeros((16, 128), F32) for _ in (0, 1)]
            totals = [[jnp.zeros((16, 128), F32) for _ in range(3)] for _ in (0, 1)]
            for index in range(27):
                slopes = near_slope[index]
                turned = [near_turned[index, 16 * c : 16 * c + 16, :] for c in range(3)]
                for j in (0, 1):
                    embed = affinity[2 * i + j, index]
                    plain[j] = plain[j] + embed * slopes
                    totals[j] = [t + embed * c for t, c in zip(totals[j], turned)]
            for j in (0, 1):
                weight = jnp.sum(plain[j], axis=0, keepdims=True)
                for c in range(3):
                    at = pl.ds(16 * c + 2 * i + j, 1)
                    force[at, :] += jnp.sum(totals[j][c], axis=0, keepdims=True) - shown[at, :] * weight
            return carry

        lax.fori_loop(0, 8, two_forces, 0)

        old = velocity[...]
        kicks = rest[pl.ds(pl.multiple_of(48 + 48 * step, 16), 48), :]
        kicked = old + 0.03 * jnp.where(live3, -2.0 * force[...], 0.0)
        noise = jnp.concatenate([level_ref[...]] * 3, axis=0)
        damped = 0.97 * kicked + noise * kicks
        gain = kicked * kicked - damped * damped
        handed[...] += jnp.where(live, 0.5 * (gain[0:16] + gain[16:32] + gain[32:48]), 0.0)
        velocity[...] = jnp.where(live3, damped, old)
        position[...] += 0.03 * jnp.where(live3, damped, 0.0)
        return carry

    lax.fori_loop(0, STEPS, dynamics, 0)

    back_out[0:48, :] = position[...]
    back_out[48:96, :] = velocity[...]

    entry = rest[144:160, :]
    placed = []
    for bx, bz in itertools.product((0, 1), repeat=2):
        low, high = (
            jnp.sum(
                jnp.where(entry == float(4 * bx + 2 * by + bz), handed[...], 0.0), axis=0, keepdims=True
            )
            for by in (0, 1)
        )
        rows_y = jnp.where((row & 1) == 1, high, low)
        placed.append(jnp.where((row >> 1) == ((lane >> 4) & 3), rows_y, 0.0))
    deposit = jnp.dot(
        jnp.concatenate(placed, axis=1), choice[...],
        precision=lax.Precision.HIGHEST, preferred_element_type=F32,
    )

    fold, place = lane >> 6, lane & 63
    depth = (lax.broadcasted_iota(jnp.int32, (24, 128), 1) & 63) + (32 * tz - 16)
    inner_face = (depth >= 0) & (depth < 255)

    def extend(tile_of, put):
        for i in range(FOLD):
            for yt in (-1, 0, 1):
                halves = []
                for h, x in ((0, i - HALO), (1, 3 + HALO - i)):
                    xt, xi = x // 4, x % 4
                    low, mid, high = (
                        turn(tile_of((xt, yt, zt)), 64 * h + 16 + 32 * zt - 32 * xi) for zt in (-1, 0, 1)
                    )
                    halves.append(jnp.where(place < 16, low, jnp.where(place < 48, mid, high)))
                put(i, 8 * yt + 8, jnp.where(fold == 0, halves[0], halves[1]))

    def conduct(t):
        square = 1.0 + t * t
        inverse = pl.reciprocal(square, approx=True)
        return 2.0 - inverse * (2.0 - square * inverse)

    def sweep(start):
        last = ext[start - 1]
        here = ext[start]
        k_here = conduct(here)
        before = (conduct(last) + k_here) * (here - last)
        for i in range(start, FOLD):
            if i < FOLD - 1:
                ahead = ext[i + 1]
                k_ahead = conduct(ahead)
            else:
                ahead, k_ahead = turn(here, 64), turn(k_here, 64)
            after = (k_here + k_ahead) * (ahead - here)
            up_y = (k_here + turn(k_here, -1, 0)) * (turn(here, -1, 0) - here)
            up_z = (k_here + turn(k_here, -1)) * (turn(here, -1) - here)
            up_z = jnp.where(inner_face, up_z, 0.0)
            net = (after - before) + (up_y - turn(up_y, 1, 0)) + (up_z - turn(up_z, 1))
            ext[i] = here + 0.04 * net + ext_src[i]
            before, here, k_here = after, ahead, k_ahead

    def centre():
        tile = None
        for x in range(4):
            h = x // 2
            moved = turn(ext[HALO + (x if h == 0 else 3 - x), 8:16, :], 32 * x - 64 * h - 16)
            tile = moved if tile is None else jnp.where((lane >> 5) == x, moved, tile)
        return tile

    def put_level(i, at, block):
        ext[i, at : at + 8, :] = block

    decay = (lane & 63).astype(F32) + ((32 * tz).astype(F32) - 15.5)
    decay = 0.02 * jnp.exp(decay * (-1.0 / 64.0))

    def put_source(i, at, block):
        ext_src[i, at : at + 8, :] = block * decay

    for turn_of in range(ROUNDS):
        out, land = tile_out.at[turn_of], tile_land.at[turn_of]
        if turn_of == 0:
            out[...] = heat[:, 0, :] + 0.5 * deposit
        else:
            out[...] = centre()
        for index, d in enumerate(WIDE):
            there = WIDE.index(tuple(-c for c in d))
            send(out, land.at[there], tile_sem.at[turn_of], partner(d))
        if turn_of == 0:
            send(back_out, back_land, back_sem, owner(tz))
            take(laser_land, laser_sem.at[1])

            def laser_of(d):
                d = (d[0], d[1], 0)
                return laser_out[...] if d == (0, 0, 0) else laser_land[FLAT.index(d)]

            extend(laser_of, put_source)
        if turn_of == ROUNDS - 1:
            take(back_land, back_sem.at[1])
            for ref, at in ((position_out, 0), (velocity_out, 48)):
                for c in range(3):
                    block = back_land[at + 16 * c : at + 16 * c + 16, :]
                    for k in range(8):
                        ref[pl.ds(128 * c + k, 16, stride=8), :] = block[:, 16 * k : 16 * k + 16]
        take(land, tile_sem.at[turn_of, 1])
        extend(lambda d: out[...] if d == (0, 0, 0) else land[WIDE.index(d)], put_level)
        for start in range(1, HALO + 1):
            sweep(start)

    result = centre()
    for y in range(8):
        row_out[y, :, :] = result[y : y + 1]
        send(row_out.at[y], row_land.at[tz], row_sem, owner(y))

    take(first_ref, first_sem.at[0, 0])
    take(rest_ref, first_sem.at[1, 0])
    take(heat_ref, heat_sem.at[0])
    for step in range(STEPS):
        take(pos_land.at[step], pos_sem.at[step, 0])
        take(slope_land.at[step], slope_sem.at[step, 0])
    take(laser_land, laser_sem.at[0])
    for turn_of in range(ROUNDS):
        take(tile_land.at[turn_of], tile_sem.at[turn_of, 0])
    take(back_out, back_sem.at[0])
    take(row_out, row_sem.at[0])

    take(row_land, row_sem.at[1])
    rows = row_land[:, 0, :]
    for x in range(4):
        line = jnp.zeros((8, 128), F32)
        for k in range(4):
            line = jnp.where(
                ((row & 3) == k) & ((lane >> 5) == k), turn(rows, 32 * k - 32 * x), line
            )
        level_out[x, :, 0:128] = jnp.sum(line[0:4], axis=0, keepdims=True)
        level_out[x, :, 128:256] = jnp.sum(line[4:8], axis=0, keepdims=True)


def face_rows(pieces):
    return 8 * (pieces + 2 + 2 * ((pieces + 3) // 4))


def shards(
    particle_local_offsets,
    particle_velocity,
    stochastic_kicks,
    thermal_mesh_entry,
    occupant_tally,
    fermion_thermal_level,
    fluence_profile,
):
    vmem = pl.BlockSpec(memory_space=pltpu.VMEM)
    buffers = [
        (56, 128), (160, 128), (8, 2, 128),
        (56, 128), (160, 128), (8, 2, 128), (48, 128), (48, 128), (48, 128),
        (27, 48, 128), (27, 16, 128), (27, 48, 128), (16, 128), (48, 128),
        (16, 27, 16, 128), (STEPS, face_rows(6), 128), (STEPS, POS_TOTAL, 128),
        (STEPS, face_rows(2), 128), (STEPS, SLOPE_TOTAL, 128), (16, 128), (16, 128), (512, 128),
        (ROUNDS, 8, 128), (ROUNDS, len(WIDE), 8, 128), (8, 128), (len(FLAT), 8, 128),
        (FOLD, 24, 128), (FOLD, 24, 128),
        (96, 128), (96, 128), (8, 1, 128), (8, 1, 128),
    ]
    sems = [(2, 2), (2,), (STEPS, 2), (STEPS, 2), (ROUNDS, 2), (2,), (2,), (2,)]
    position, velocity, level = pl.pallas_call(
        kernel,
        out_shape=(
            jax.ShapeDtypeStruct((384, 16), F32),
            jax.ShapeDtypeStruct((384, 16), F32),
            jax.ShapeDtypeStruct(fermion_thermal_level.shape, F32),
        ),
        in_specs=[vmem] * 7,
        out_specs=(vmem, vmem, vmem),
        scratch_shapes=[pltpu.VMEM(shape, F32) for shape in buffers]
        + [pltpu.SemaphoreType.DMA(shape) for shape in sems],
        compiler_params=pltpu.CompilerParams(
            collective_id=0, has_side_effects=True, vmem_limit_bytes=32 * 1024 * 1024
        ),
    )(
        particle_local_offsets.reshape(384, 16),
        particle_velocity.reshape(384, 16),
        stochastic_kicks.reshape(768, 16),
        thermal_mesh_entry.reshape(128, 16),
        occupant_tally,
        fermion_thermal_level,
        fluence_profile.T,
    )
    shape = particle_local_offsets.shape
    return position.reshape(shape), velocity.reshape(shape), level


def solution(mesh):
    placed = (
        P(None, None, "gx", "gy", "gz"),
        P(None, None, "gx", "gy", "gz"),
        P(None, None, None, "gx", "gy", "gz"),
        P(None, "gx", "gy", "gz"),
        P("gx", "gy", "gz"),
        P("gx", ("gy", "gz"), None),
        P("gx", ("gy", "gz")),
    )
    return jax.shard_map(
        shards,
        mesh=mesh,
        in_specs=placed,
        out_specs=(
            P(None, None, "gx", "gy", "gz"),
            P(None, None, "gx", "gy", "gz"),
            P("gx", ("gy", "gz"), None),
        ),
        check_vma=False,
    )
```

time: 103 us -> 83.8 us (0.81)
  Pallas kernels: 92.7 us -> 76.6 us
  other arithmetic: 2.88 us -> 0 us
    pallas_call x1, Pallas kernels: 92.7 us -> 76.6 us  [shards(): pl.pallas_call(kernel, out_shape=(jax.ShapeDtypeStruct((384, 16), F32), j...]
    unnamed x4 -> x17, local copies, waits for them, and re-layouts: 0.56 us -> 6.32 us
    reshape x9 -> x0, local copies, waits for them, and re-layouts: 5.12 us -> none  [the longest x2 1.72 us: shards(): return (moved[:48].reshape(shape), moved[48:].reshape(shape), grid)]
where the time goes in v2:
time: 83.8 us; the launch traced here: 83.5 us
  Pallas kernels  76.6 us (91%)
  local copies, waits for them, and re-layouts  6.32 us (8%)
    pallas_call x1, Pallas kernels, shards(): pl.pallas_call(kernel, out_shape=(jax.ShapeDtypeStruct((384, 16), F32), j...  76.6 us
    unnamed x17, local copies, waits for them, and re-layouts  6.32 us

profile of v2, /device:TPU:5, one launch (start us, length us, event | category | flops | bytes accessed | tf_op | source)
XLA Modules:
  0.0 83.5 jit_solution(12882975745351881500)
XLA Ops:
  0.6 0.0 copy-start.5
  0.6 0.0 copy-start.4
  0.7 0.0 copy-start.6
  0.7 0.7 copy-done.5
  1.3 0.0 copy-done.4
  1.3 0.0 copy-done.6
  1.3 0.0 copy-start
  1.3 1.0 %copy-done = f32[2,3,16,2,4,16]{5,4,3,2,1,0:T(4,128)S(1)} copy-done((f32[2,3,16,2,4,16]{5,4,3,2,1,0:T(4,128)S(1)}, f32[2,3,16,2,4,16]{5,4,3,2,1,0:T(4,128)}, u32[]{:S(2)}) %copy-start) | copy-done | bytes 49176
  2.3 0.0 copy-start.1
  2.3 0.9 %copy-done.1 = f32[3,16,2,4,16]{4,3,2,1,0:T(4,128)S(1)} copy-done((f32[3,16,2,4,16]{4,3,2,1,0:T(4,128)S(1)}, f32[3,16,2,4,16]{4,3,2,1,0:T(4,128)}, u32[]{:S(2)}) %copy-start.1) | copy-done | bytes 24600
  3.3 0.0 copy-start.2
  3.3 0.9 %copy-done.2 = f32[3,16,2,4,16]{4,3,2,1,0:T(4,128)S(1)} copy-done((f32[3,16,2,4,16]{4,3,2,1,0:T(4,128)S(1)}, f32[3,16,2,4,16]{4,3,2,1,0:T(4,128)}, u32[]{:S(2)}) %copy-start.2) | copy-done | bytes 24600
  4.2 0.0 copy-start.3
  4.2 0.8 %copy-done.3 = s32[16,2,4,16]{3,2,1,0:T(4,128)S(1)} copy-done((s32[16,2,4,16]{3,2,1,0:T(4,128)S(1)}, s32[16,2,4,16]{3,2,1,0:T(4,128)}, u32[]{:S(2)}) %copy-start.3) | copy-done | bytes 8216
  5.0 76.6 %shard_map.94 = (f32[384,16]{1,0:T(8,128)S(1)}, f32[384,16]{1,0:T(8,128)S(1)}, f32[4,1,256]{2,1,0:T(1,128)S(1)}) custom-call(f32[384,16]{1,0:T(8,128)S(1)} %bitcast.10, f32[384,16]{1,0:T(8,128)S(1)} %bitcast.11, f32[768,16]{1,0:T(8,128)S(1)} %bitcast.7, s32[128,16]{1,0:T(8,128)S(1)} %bitcast.12, s32[2,4,16]{2,1,0:T(4,128)S(1)} %copy-done.4, ...), custom_call_target="tpu_custom_call" | custom-call | tf_op jit(solution)/shard_map/pallas_call | solution.py:563
  81.6 0.7 copy.13
  82.3 0.7 copy.14
  83.0 0.6 copy.15
Async XLA Ops:
  0.6 0.7 copy-start.5
  0.6 0.7 copy-start.4
  0.7 0.7 copy-start.6
  1.3 1.0 %copy-start = (f32[2,3,16,2,4,16]{5,4,3,2,1,0:T(4,128)S(1)}, f32[2,3,16,2,4,16]{5,4,3,2,1,0:T(4,128)}, u32[]{:S(2)}) copy-start(f32[2,3,16,2,4,16]{5,4,3,2,1,0:T(4,128)} %param.9) | copy-start | bytes 147460
  2.3 0.9 %copy-start.1 = (f32[3,16,2,4,16]{4,3,2,1,0:T(4,128)S(1)}, f32[3,16,2,4,16]{4,3,2,1,0:T(4,128)}, u32[]{:S(2)}) copy-start(f32[3,16,2,4,16]{4,3,2,1,0:T(4,128)} %param.7) | copy-start | bytes 73732
  3.3 0.9 %copy-start.2 = (f32[3,16,2,4,16]{4,3,2,1,0:T(4,128)S(1)}, f32[3,16,2,4,16]{4,3,2,1,0:T(4,128)}, u32[]{:S(2)}) copy-start(f32[3,16,2,4,16]{4,3,2,1,0:T(4,128)} %param.8) | copy-start | bytes 73732
  4.2 0.8 %copy-start.3 = (s32[16,2,4,16]{3,2,1,0:T(4,128)S(1)}, s32[16,2,4,16]{3,2,1,0:T(4,128)}, u32[]{:S(2)}) copy-start(s32[16,2,4,16]{3,2,1,0:T(4,128)} %param.10) | copy-start | bytes 24580

commit v3 on v2

--- a/solution.py
+++ b/solution.py
@@ -148,30 +148,42 @@
 
 
 def kernel(
+    position_arg, velocity_arg, kicks_arg, entry_arg, tally_arg, level_arg, fluence_arg,
+    position_out, velocity_out, level_out,
     position_ref, velocity_ref, kicks_ref, entry_ref, tally_ref, level_in, fluence_ref,
-    position_out, velocity_out, level_out,
     first_ref, rest_ref, heat_ref,
     first, rest, heat, position, velocity, shown, near, near_slope, near_turned, density, force,
     affinity, pos_face, pos_land, slope_face, slope_land, level_ref, handed, choice,
     tile_out, tile_land, laser_out, laser_land, ext, ext_src,
     back_out, back_land, row_out, row_land,
-    first_sem, heat_sem, pos_sem, slope_sem, tile_sem, laser_sem, back_sem, row_sem,
+    input_sem, first_sem, heat_sem, pos_sem, slope_sem, tile_sem, laser_sem, back_sem, row_sem,
 ):
+    inputs = [
+        pltpu.make_async_copy(arg, ref, input_sem.at[k])
+        for k, (arg, ref) in enumerate(
+            [
+                (position_arg, position_ref), (tally_arg, tally_ref), (level_arg, level_in),
+                (fluence_arg, fluence_ref), (velocity_arg, velocity_ref), (kicks_arg, kicks_ref),
+                (entry_arg, entry_ref),
+            ]
+        )
+    ]
+    for copy in inputs:
+        copy.start()
     gx, gy, gz = (lax.axis_index(a) for a in ("gx", "gy", "gz"))
 
     def x_place(tx):
-        ring = lax.rem(tx + 1, 8)
-        return lax.rem(ring, 2), (ring // 2) * 2
+        y = lax.rem(tx + 4, 8)
+        return lax.rem(y, 4) * 2, y // 4
 
     def y_place(ty):
-        return lax.rem(ty, 4) * 2, ty // 4
+        return lax.rem(ty, 2), (ty // 2) * 2
 
     def device(xp, yp, tz):
         return (xp[0] + yp[0], xp[1] + yp[1], tz)
 
-    ring_place = (gy // 2) * 2 + lax.rem(gx, 2)
-    tx = lax.rem(ring_place + 7, 8)
-    ty = lax.rem(gy, 2) * 4 + gx // 2
+    tx = lax.rem(lax.rem(gy, 2) * 4 + gx // 2 + 4, 8)
+    ty = (gy // 2) * 2 + lax.rem(gx, 2)
     tz = gz
     xs = {d: x_place(lax.rem(tx + d + 8, 8)) for d in range(-2, 3)}
     ys = {d: y_place(lax.rem(ty + d + 8, 8)) for d in (-1, 0, 1)}
@@ -201,10 +213,26 @@
     def by_lane(ref, base):
         return jnp.concatenate([ref[pl.ds(base + k, 16, stride=8), :] for k in range(8)], axis=1)
 
+    inputs[0].wait()
+    inputs[1].wait()
     for c in range(3):
         first_ref[16 * c : 16 * c + 16, :] = by_lane(position_ref, 128 * c)
     tally = jnp.concatenate([tally_ref[k // 4, k % 4 : k % 4 + 1, :] for k in range(8)], axis=1)
     first_ref[48:56, :] = jnp.broadcast_to(tally.astype(F32), (8, 128))
+    pl.semaphore_wait(barrier, len(greeted))
+
+    def send(src, dst, sems, target):
+        pltpu.make_async_remote_copy(
+            src_ref=src, dst_ref=dst, send_sem=sems.at[0], recv_sem=sems.at[1],
+            device_id=target, device_id_type=MESH,
+        ).start()
+
+    def take(ref, sem):
+        pltpu.make_async_copy(ref, ref, sem).wait()
+
+    send(first_ref, first, first_sem.at[0], worker(gz))
+    inputs[2].wait()
+    inputs[3].wait()
     warm, fluence = jnp.zeros((8, 128), F32), jnp.zeros((8, 128), F32)
     for x in range(4):
         upper = jnp.broadcast_to(level_in[x, :, 0:128], (8, 128))
@@ -215,27 +243,15 @@
         fluence = jnp.where((lane >> 5) == x, fluence_ref[0:1, x : x + 1], fluence)
     heat_ref[:, 0, :] = warm
     heat_ref[:, 1, :] = fluence
-
-    pl.semaphore_wait(barrier, len(greeted))
-
-    def send(src, dst, sems, target):
-        pltpu.make_async_remote_copy(
-            src_ref=src, dst_ref=dst, send_sem=sems.at[0], recv_sem=sems.at[1],
-            device_id=target, device_id_type=MESH,
-        ).start()
-
-    def take(ref, sem):
-        pltpu.make_async_copy(ref, ref, sem).wait()
-
-    send(first_ref, first, first_sem.at[0], worker(gz))
     for z in range(8):
         send(heat_ref.at[z], heat.at[gz], heat_sem, worker(z))
+    for copy in inputs[4:]:
+        copy.wait()
     for c in range(3):
         rest_ref[16 * c : 16 * c + 16, :] = by_lane(velocity_ref, 128 * c)
     for c in range(6):
         rest_ref[48 + 16 * c : 64 + 16 * c, :] = by_lane(kicks_ref, 128 * c)
     rest_ref[144:160, :] = by_lane(entry_ref, 0).astype(F32)
-    send(rest_ref, rest, first_sem.at[1], worker(gz))
 
     target = lax.broadcasted_iota(jnp.int32, (128, 128), 0)
     source = lax.broadcasted_iota(jnp.int32, (128, 128), 1)
@@ -274,6 +290,10 @@
             shown[8 * k : 8 * k + 8, :] = piece
         spread(own, packed(own), pos_face.at[step], pos_land.at[step], POS_ROWS, pos_sem.at[step])
         take(pos_land.at[step], pos_sem.at[step, 1])
+
+        @pl.when(step == 0)
+        def _():
+            send(rest_ref, rest, first_sem.at[1], worker(gz))
 
         def put_position(e, pieces):
             index = CUBE.index(e)
@@ -549,6 +569,15 @@
     fluence_profile,
 ):
     vmem = pl.BlockSpec(memory_space=pltpu.VMEM)
+    args = (
+        particle_local_offsets.reshape(384, 16),
+        particle_velocity.reshape(384, 16),
+        stochastic_kicks.reshape(768, 16),
+        thermal_mesh_entry.reshape(128, 16),
+        occupant_tally,
+        fermion_thermal_level,
+        fluence_profile.T,
+    )
     buffers = [
         (56, 128), (160, 128), (8, 2, 128),
         (56, 128), (160, 128), (8, 2, 128), (48, 128), (48, 128), (48, 128),
@@ -559,7 +588,7 @@
         (FOLD, 24, 128), (FOLD, 24, 128),
         (96, 128), (96, 128), (8, 1, 128), (8, 1, 128),
     ]
-    sems = [(2, 2), (2,), (STEPS, 2), (STEPS, 2), (ROUNDS, 2), (2,), (2,), (2,)]
+    sems = [(7,), (2, 2), (2,), (STEPS, 2), (STEPS, 2), (ROUNDS, 2), (2,), (2,), (2,)]
     position, velocity, level = pl.pallas_call(
         kernel,
         out_shape=(
@@ -567,22 +596,15 @@
             jax.ShapeDtypeStruct((384, 16), F32),
             jax.ShapeDtypeStruct(fermion_thermal_level.shape, F32),
         ),
-        in_specs=[vmem] * 7,
+        in_specs=[pl.BlockSpec(memory_space=pltpu.HBM)] * 7,
         out_specs=(vmem, vmem, vmem),
-        scratch_shapes=[pltpu.VMEM(shape, F32) for shape in buffers]
+        scratch_shapes=[pltpu.VMEM(arg.shape, arg.dtype) for arg in args]
+        + [pltpu.VMEM(shape, F32) for shape in buffers]
         + [pltpu.SemaphoreType.DMA(shape) for shape in sems],
         compiler_params=pltpu.CompilerParams(
-            collective_id=0, has_side_effects=True, vmem_limit_bytes=32 * 1024 * 1024
+            collective_id=0, has_side_effects=True, vmem_limit_bytes=60 * 1024 * 1024
         ),
-    )(
-        particle_local_offsets.reshape(384, 16),
-        particle_velocity.reshape(384, 16),
-        stochastic_kicks.reshape(768, 16),
-        thermal_mesh_entry.reshape(128, 16),
-        occupant_tally,
-        fermion_thermal_level,
-        fluence_profile.T,
-    )
+    )(*args)
     shape = particle_local_offsets.shape
     return position.reshape(shape), velocity.reshape(shape), level
 

time: 83.8 us -> 76.1 us (0.908)
  the two profiles are of different devices: /device:TPU:5 before, /device:TPU:1 now
where the time goes in v3:
time: 76.1 us; the launch traced here: 75.9 us
  Pallas kernels  72.3 us (95%)
  local copies, waits for them, and re-layouts  2.94 us (4%)
    pallas_call x1, Pallas kernels, shards(): pl.pallas_call(kernel, out_shape=(jax.ShapeDtypeStruct((384, 16), F32), j...  72.3 us
    unnamed x7, local copies, waits for them, and re-layouts  2.94 us

profile of v3, /device:TPU:1, one launch (start us, length us, event | category | flops | bytes accessed | tf_op | source)
XLA Modules:
  0.0 75.9 jit_solution(7227894224665604468)
XLA Ops:
  0.6 72.3 %shard_map.94 = (f32[384,16]{1,0:T(8,128)}, f32[384,16]{1,0:T(8,128)}, f32[4,1,256]{2,1,0:T(1,128)}) custom-call(f32[384,16]{1,0:T(8,128)} %bitcast.10, f32[384,16]{1,0:T(8,128)} %bitcast.11, f32[768,16]{1,0:T(8,128)} %bitcast.7, s32[128,16]{1,0:T(8,128)} %bitcast.12, s32[2,4,16]{2,1,0:T(4,128)} %tally_arg.1, f32[4,1,256]{2,1,0:T(1,128)} %level_arg.1, ...), custom_call_target="tpu_custom_call" | custom-call | tf_op jit(solution)/shard_map/pallas_call | solution.py:592
  73.0 0.0 copy-start
  73.0 1.7 %copy.13 = f32[3,16,2,4,16]{4,3,2,1,0:T(4,128)} copy(f32[3,16,2,4,16]{4,3,2,1,0:T(4,128)} %bitcast.9) | data formatting | bytes 49152
  74.7 0.0 copy-done
  74.7 0.0 copy-start.1
  74.7 0.7 copy.14
  75.3 0.0 copy-done.1
  75.3 0.6 copy.15
Async XLA Ops:
  73.0 1.7 %copy-start = (f32[384,16]{1,0:T(8,128)S(1)}, f32[384,16]{1,0:T(8,128)}, u32[]{:S(2)}) copy-start(f32[384,16]{1,0:T(8,128)} %get-tuple-element.7) | copy-start | bytes 73732
  74.7 0.7 copy-start.1

commit v4 on v3

--- a/solution.py
+++ b/solution.py
@@ -1,4 +1,5 @@
 import itertools
+import math
 
 import jax
 import jax.numpy as jnp
@@ -13,6 +14,8 @@
 HALO = 8
 ROUNDS = 16 // HALO
 REACH = HALO // 4
+RANGE = 2.0 * math.log2(math.e)
+UNIT = math.sqrt(RANGE)
 FAR = 1.0e6
 CUBE = [d for d in itertools.product((-1, 0, 1), repeat=3)]
 AROUND = sorted((d for d in CUBE if d != (0, 0, 0)), key=lambda d: -sum(map(abs, d)))
@@ -285,7 +288,7 @@
     handed[...] = jnp.zeros((16, 128), F32)
 
     def dynamics(step, carry):
-        own = pieces_of(jnp.where(live3, position[...], FAR))
+        own = pieces_of(jnp.where(live3, UNIT * position[...], FAR))
         for k, piece in enumerate(own):
             shown[8 * k : 8 * k + 8, :] = piece
         spread(own, packed(own), pos_face.at[step], pos_land.at[step], POS_ROWS, pos_sem.at[step])
@@ -298,7 +301,7 @@
         def put_position(e, pieces):
             index = CUBE.index(e)
             for k, piece in enumerate(pieces):
-                near[index, 8 * k : 8 * k + 8, :] = piece + float(e[k // 2])
+                near[index, 8 * k : 8 * k + 8, :] = piece + UNIT * e[k // 2]
 
         landed = pos_land[step]
         neighbours(own, landed, POS_ROWS, at_bottom, at_top, put_position)
@@ -311,14 +314,15 @@
                 for j in (0, 1):
                     d = [there[c] - homes[j][c] for c in range(3)]
                     q = d[0] * d[0] + d[1] * d[1] + d[2] * d[2]
-                    w = jnp.maximum(1.0 - q, 0.0)
-                    totals[j] = totals[j] + jnp.exp(-2.0 * q) * (w * w)
+                    left = RANGE - q
+                    w = jnp.maximum(left, 0.0)
+                    totals[j] = totals[j] + jnp.exp2(left) * (w * w)
             for j in (0, 1):
                 density[pl.ds(2 * i + j, 1), :] = jnp.sum(totals[j], axis=0, keepdims=True)
             return carry
 
         lax.fori_loop(0, 8, two_densities, 0)
-        rho = jnp.where(live, density[...] - 1.0, 0.0)
+        rho = jnp.where(live, math.exp(-2.0) / RANGE**2 * density[...] - 1.0, 0.0)
         slope = -10.0 * lax.rsqrt(1.0 + jnp.maximum(rho, 0.0))
         density[...] = slope
         own_slope = pieces_of(slope)
@@ -336,8 +340,8 @@
                 for j in (0, 1):
                     d = [there[c] - homes[j][c] for c in range(3)]
                     q = d[0] * d[0] + d[1] * d[1] + d[2] * d[2]
-                    w = jnp.maximum(1.0 - q, 0.0)
-                    once = jnp.exp(-q)
+                    w = jnp.maximum(RANGE - q, 0.0) * (1.0 / RANGE)
+                    once = jnp.exp2(-0.5 * q)
                     common = w * (once * once)
                     embed = common * (w + 1.0)
                     affinity[2 * i + j, index] = embed
@@ -409,7 +413,7 @@
 
         old = velocity[...]
         kicks = rest[pl.ds(pl.multiple_of(48 + 48 * step, 16), 48), :]
-        kicked = old + 0.03 * jnp.where(live3, -2.0 * force[...], 0.0)
+        kicked = old + 0.03 * jnp.where(live3, (-2.0 / UNIT) * force[...], 0.0)
         noise = jnp.concatenate([level_ref[...]] * 3, axis=0)
         damped = 0.97 * kicked + noise * kicks
         gain = kicked * kicked - damped * damped
@@ -553,6 +557,21 @@
             )
         level_out[x, :, 0:128] = jnp.sum(line[0:4], axis=0, keepdims=True)
         level_out[x, :, 128:256] = jnp.sum(line[4:8], axis=0, keepdims=True)
+
+
+def deliver(*refs):
+    sources, results, stops, sem = refs[:3], refs[3:6], refs[6:9], refs[9]
+    copies = [
+        [pltpu.make_async_copy(src, dst, sem.at[leg, k]) for k, (src, dst) in enumerate(pairs)]
+        for leg, pairs in enumerate((zip(sources, stops), zip(stops, results)))
+    ]
+    for copy in copies[0]:
+        copy.start()
+    for copy, onward in zip(*copies):
+        copy.wait()
+        onward.start()
+    for copy in copies[1]:
+        copy.wait()
 
 
 def face_rows(pieces):
@@ -605,6 +624,16 @@
             collective_id=0, has_side_effects=True, vmem_limit_bytes=60 * 1024 * 1024
         ),
     )(*args)
+    results = (position, velocity, level)
+    position, velocity, level = pl.pallas_call(
+        deliver,
+        out_shape=tuple(jax.ShapeDtypeStruct(result.shape, F32) for result in results),
+        in_specs=[pl.BlockSpec(memory_space=pltpu.HBM)] * 3,
+        out_specs=(pl.BlockSpec(memory_space=pltpu.HBM),) * 3,
+        scratch_shapes=[pltpu.VMEM(result.shape, F32) for result in results]
+        + [pltpu.SemaphoreType.DMA((2, 3))],
+        compiler_params=pltpu.CompilerParams(vmem_limit_bytes=60 * 1024 * 1024),
+    )(*results)
     shape = particle_local_offsets.shape
     return position.reshape(shape), velocity.reshape(shape), level
 

time: 76.1 us -> 74.4 us (0.978)
  local copies, waits for them, and re-layouts: 2.94 us -> 0 us
  Pallas kernels: 72.3 us -> 73.6 us
    unnamed x7 -> x0, local copies, waits for them, and re-layouts: 2.94 us -> none
    pallas_call x0 -> x1, Pallas kernels: none -> 1.75 us  [shards(): pl.pallas_call(deliver, out_shape=tuple((jax.ShapeDtypeStruct(result.shap...]
where the time goes in v4:
time: 74.4 us; the launch traced here: 74.2 us
  Pallas kernels  73.6 us (99%)
    pallas_call x1, Pallas kernels, shards(): pl.pallas_call(kernel, out_shape=(jax.ShapeDtypeStruct((384, 16), F32), j...  71.9 us
    pallas_call x1, Pallas kernels, shards(): pl.pallas_call(deliver, out_shape=tuple((jax.ShapeDtypeStruct(result.shap...  1.75 us

profile of v4, /device:TPU:1, one launch (start us, length us, event | category | flops | bytes accessed | tf_op | source)
XLA Modules:
  0.0 74.2 jit_solution(2986989813038708329)
XLA Ops:
  0.6 71.9 %shard_map.94 = (f32[384,16]{1,0:T(8,128)}, f32[384,16]{1,0:T(8,128)}, f32[4,1,256]{2,1,0:T(1,128)}) custom-call(f32[384,16]{1,0:T(8,128)} %bitcast.8, f32[384,16]{1,0:T(8,128)} %bitcast.9, f32[768,16]{1,0:T(8,128)} %bitcast.7, s32[128,16]{1,0:T(8,128)} %bitcast.10, s32[2,4,16]{2,1,0:T(4,128)} %tally_arg.1, f32[4,1,256]{2,1,0:T(1,128)} %level_arg.1, ...), custom_call_target="tpu_custom_call" | custom-call | tf_op jit(solution)/shard_map/pallas_call | solution.py:611
  72.5 1.8 %shard_map.95 = (f32[384,16]{1,0:T(8,128)}, f32[384,16]{1,0:T(8,128)}, f32[4,1,256]{2,1,0:T(1,128)}) custom-call(f32[384,16]{1,0:T(8,128)} %get-tuple-element.9.refs_0_, f32[384,16]{1,0:T(8,128)} %get-tuple-element.10.refs_1_, f32[4,1,256]{2,1,0:T(1,128)} %get-tuple-element.11.refs_2_), custom_call_target="tpu_custom_call" | custom-call | tf_op jit(solution)/shard_map/pallas_call | solution.py:628

commit v5 on v4

--- a/solution.py
+++ b/solution.py
@@ -154,15 +154,18 @@
     position_arg, velocity_arg, kicks_arg, entry_arg, tally_arg, level_arg, fluence_arg,
     position_out, velocity_out, level_out,
     position_ref, velocity_ref, kicks_ref, entry_ref, tally_ref, level_in, fluence_ref,
-    first_ref, rest_ref, heat_ref,
-    first, rest, heat, position, velocity, shown, near, near_slope, near_turned, density, force,
+    position_stage, velocity_stage, first_ref, rest_ref, heat_ref,
+    first, rest, heat, position, velocity, shown, near, beside, beyond, near_slope, near_turned, density, force,
     affinity, pos_face, pos_land, slope_face, slope_land, level_ref, handed, choice,
     tile_out, tile_land, laser_out, laser_land, ext, ext_src,
     back_out, back_land, row_out, row_land,
     input_sem, first_sem, heat_sem, pos_sem, slope_sem, tile_sem, laser_sem, back_sem, row_sem,
 ):
     inputs = [
-        pltpu.make_async_copy(arg, ref, input_sem.at[k])
+        pltpu.make_async_copy(
+            arg, ref.at[pl.ds(0, arg.shape[0])] if len(arg.shape) == 2 and arg.shape[0] > 8 else ref,
+            input_sem.at[k],
+        )
         for k, (arg, ref) in enumerate(
             [
                 (position_arg, position_ref), (tally_arg, tally_ref), (level_arg, level_in),
@@ -285,6 +288,7 @@
                 sems, partner(d),
             )
 
+    tall = lax.broadcasted_iota(jnp.int32, (48, 128), 1)
     handed[...] = jnp.zeros((16, 128), F32)
 
     def dynamics(step, carry):
@@ -292,36 +296,76 @@
         for k, piece in enumerate(own):
             shown[8 * k : 8 * k + 8, :] = piece
         spread(own, packed(own), pos_face.at[step], pos_land.at[step], POS_ROWS, pos_sem.at[step])
-        take(pos_land.at[step], pos_sem.at[step, 1])
-
-        @pl.when(step == 0)
-        def _():
-            send(rest_ref, rest, first_sem.at[1], worker(gz))
 
         def put_position(e, pieces):
             index = CUBE.index(e)
             for k, piece in enumerate(pieces):
                 near[index, 8 * k : 8 * k + 8, :] = piece + UNIT * e[k // 2]
 
+        def sum_densities(there_ref, count, more):
+            def two_densities(i, carry):
+                homes = [[shown[pl.ds(16 * c + 2 * i + j, 1), :] for c in range(3)] for j in (0, 1)]
+                totals = [jnp.zeros((16, 128), F32) for _ in (0, 1)]
+                for index in range(count):
+                    there = [there_ref[index, 16 * c : 16 * c + 16, :] for c in range(3)]
+                    for j in (0, 1):
+                        d = [there[c] - homes[j][c] for c in range(3)]
+                        q = d[0] * d[0] + d[1] * d[1] + d[2] * d[2]
+                        left = RANGE - q
+                        w = jnp.maximum(left, 0.0)
+                        totals[j] = totals[j] + jnp.exp2(left) * (w * w)
+                for j in (0, 1):
+                    at = pl.ds(2 * i + j, 1)
+                    total = jnp.sum(totals[j], axis=0, keepdims=True)
+                    density[at, :] = density[at, :] + total if more else total
+                return carry
+
+            lax.fori_loop(0, 8, two_densities, 0)
+
+        empty = jnp.full((POS_TOTAL, 128), FAR, F32)
+        neighbours(own, empty, POS_ROWS, None, None, put_position)
+        sum_densities(near, 27, False)
+        take(pos_land.at[step], pos_sem.at[step, 1])
+
+        @pl.when(step == 0)
+        def _():
+            send(rest_ref, rest, first_sem.at[1], worker(gz))
+
         landed = pos_land[step]
         neighbours(own, landed, POS_ROWS, at_bottom, at_top, put_position)
 
-        def two_densities(i, carry):
-            homes = [[shown[pl.ds(16 * c + 2 * i + j, 1), :] for c in range(3)] for j in (0, 1)]
-            totals = [jnp.zeros((16, 128), F32) for _ in (0, 1)]
-            for index in range(27):
-                there = [near[index, 16 * c : 16 * c + 16, :] for c in range(3)]
-                for j in (0, 1):
-                    d = [there[c] - homes[j][c] for c in range(3)]
-                    q = d[0] * d[0] + d[1] * d[1] + d[2] * d[2]
-                    left = RANGE - q
-                    w = jnp.maximum(left, 0.0)
-                    totals[j] = totals[j] + jnp.exp2(left) * (w * w)
-            for j in (0, 1):
-                density[pl.ds(2 * i + j, 1), :] = jnp.sum(totals[j], axis=0, keepdims=True)
-            return carry
-
-        lax.fori_loop(0, 8, two_densities, 0)
+        low_x, low_y, high_y = (tall >> 6) == 0, ((tall >> 4) & 3) == 0, ((tall >> 4) & 3) == 3
+        low_z, high_z = (tall & 15) == 0, (tall & 15) == 15
+        for a, ey in enumerate((-1, 0, 1)):
+            for b, ez in enumerate((-1, 0, 1)):
+                plus, minus = near[CUBE.index((1, ey, ez))], near[CUBE.index((-1, ey, ez))]
+                beyond[3 * a + b] = jnp.where(low_x, minus, plus)
+                beside[3 * a + b] = jnp.where(low_x, plus, minus)
+
+        def within(half, ey, ez):
+            return near[CUBE.index((0, ey, ez))] if half == 0 else beside[3 * ey + ez + 4]
+
+        for half in (0, 1):
+            for g in (-1, 0, 1):
+                ends = jnp.where(
+                    high_z, within(half, g, 1), jnp.where(low_z, within(half, g, -1), FAR)
+                )
+                beyond[9 + 5 * half + g + 1] = jnp.where(
+                    high_y, within(half, 1, g), jnp.where(low_y, within(half, -1, g), ends)
+                )
+            level = jnp.where(
+                high_z, within(half, 0, 1), jnp.where(low_z, within(half, 0, -1), FAR)
+            )
+            beyond[9 + 5 * half + 3] = jnp.where(low_y | high_y, level, FAR)
+            inward = jnp.where(
+                high_z, within(half, 1, 1), jnp.where(low_z, within(half, 1, -1), FAR)
+            )
+            outward = jnp.where(
+                high_z, within(half, -1, 1), jnp.where(low_z, within(half, -1, -1), FAR)
+            )
+            beyond[9 + 5 * half + 4] = jnp.where(low_y, inward, jnp.where(high_y, outward, FAR))
+
+        sum_densities(beyond, 19, True)
         rho = jnp.where(live, math.exp(-2.0) / RANGE**2 * density[...] - 1.0, 0.0)
         slope = -10.0 * lax.rsqrt(1.0 + jnp.maximum(rho, 0.0))
         density[...] = slope
@@ -520,11 +564,14 @@
             extend(laser_of, put_source)
         if turn_of == ROUNDS - 1:
             take(back_land, back_sem.at[1])
-            for ref, at in ((position_out, 0), (velocity_out, 48)):
+            for ref, at in ((position_stage, 0), (velocity_stage, 48)):
                 for c in range(3):
                     block = back_land[at + 16 * c : at + 16 * c + 16, :]
                     for k in range(8):
                         ref[pl.ds(128 * c + k, 16, stride=8), :] = block[:, 16 * k : 16 * k + 16]
+        if turn_of == ROUNDS - 1:
+            position_out[...] = position_stage[0:384, :]
+            velocity_out[...] = velocity_stage[0:384, :]
         take(land, tile_sem.at[turn_of, 1])
         extend(lambda d: out[...] if d == (0, 0, 0) else land[WIDE.index(d)], put_level)
         for start in range(1, HALO + 1):
@@ -600,7 +647,7 @@
     buffers = [
         (56, 128), (160, 128), (8, 2, 128),
         (56, 128), (160, 128), (8, 2, 128), (48, 128), (48, 128), (48, 128),
-        (27, 48, 128), (27, 16, 128), (27, 48, 128), (16, 128), (48, 128),
+        (27, 48, 128), (9, 48, 128), (19, 48, 128), (27, 16, 128), (27, 48, 128), (16, 128), (48, 128),
         (16, 27, 16, 128), (STEPS, face_rows(6), 128), (STEPS, POS_TOTAL, 128),
         (STEPS, face_rows(2), 128), (STEPS, SLOPE_TOTAL, 128), (16, 128), (16, 128), (512, 128),
         (ROUNDS, 8, 128), (ROUNDS, len(WIDE), 8, 128), (8, 128), (len(FLAT), 8, 128),
@@ -617,7 +664,9 @@
         ),
         in_specs=[pl.BlockSpec(memory_space=pltpu.HBM)] * 7,
         out_specs=(vmem, vmem, vmem),
-        scratch_shapes=[pltpu.VMEM(arg.shape, arg.dtype) for arg in args]
+        scratch_shapes=[pltpu.VMEM((arg.shape[0] + 8, 16), arg.dtype) for arg in args[:4]]
+        + [pltpu.VMEM(arg.shape, arg.dtype) for arg in args[4:]]
+        + [pltpu.VMEM((392, 16), F32)] * 2
         + [pltpu.VMEM(shape, F32) for shape in buffers]
         + [pltpu.SemaphoreType.DMA(shape) for shape in sems],
         compiler_params=pltpu.CompilerParams(

time: 74.4 us -> 73.6 us (0.989)
  Pallas kernels: 73.6 us -> 72.8 us
    pallas_call x1, Pallas kernels: 71.9 us -> 71 us  [shards(): pl.pallas_call(kernel, out_shape=(jax.ShapeDtypeStruct((384, 16), F32), j...]
where the time goes in v5:
time: 73.6 us; the launch traced here: 73.4 us
  Pallas kernels  72.8 us (99%)
    pallas_call x1, Pallas kernels, shards(): pl.pallas_call(kernel, out_shape=(jax.ShapeDtypeStruct((384, 16), F32), j...  71 us
    pallas_call x1, Pallas kernels, shards(): pl.pallas_call(deliver, out_shape=tuple((jax.ShapeDtypeStruct(result.shap...  1.75 us

profile of v5, /device:TPU:1, one launch (start us, length us, event | category | flops | bytes accessed | tf_op | source)
XLA Modules:
  0.0 73.4 jit_solution(7516030093778415466)
XLA Ops:
  0.6 71.0 %shard_map.94 = (f32[384,16]{1,0:T(8,128)}, f32[384,16]{1,0:T(8,128)}, f32[4,1,256]{2,1,0:T(1,128)}) custom-call(f32[384,16]{1,0:T(8,128)} %bitcast.8, f32[384,16]{1,0:T(8,128)} %bitcast.9, f32[768,16]{1,0:T(8,128)} %bitcast.7, s32[128,16]{1,0:T(8,128)} %bitcast.10, s32[2,4,16]{2,1,0:T(4,128)} %tally_arg.1, f32[4,1,256]{2,1,0:T(1,128)} %level_arg.1, ...), custom_call_target="tpu_custom_call" | custom-call | tf_op jit(solution)/shard_map/pallas_call | solution.py:658
  71.7 1.8 %shard_map.95 = (f32[384,16]{1,0:T(8,128)}, f32[384,16]{1,0:T(8,128)}, f32[4,1,256]{2,1,0:T(1,128)}) custom-call(f32[384,16]{1,0:T(8,128)} %get-tuple-element.9.refs_0_, f32[384,16]{1,0:T(8,128)} %get-tuple-element.10.refs_1_, f32[4,1,256]{2,1,0:T(1,128)} %get-tuple-element.11.refs_2_), custom_call_target="tpu_custom_call" | custom-call | tf_op jit(solution)/shard_map/pallas_call | solution.py:677

commit v6 on v5

--- a/solution.py
+++ b/solution.py
@@ -159,7 +159,7 @@
     affinity, pos_face, pos_land, slope_face, slope_land, level_ref, handed, choice,
     tile_out, tile_land, laser_out, laser_land, ext, ext_src,
     back_out, back_land, row_out, row_land,
-    input_sem, first_sem, heat_sem, pos_sem, slope_sem, tile_sem, laser_sem, back_sem, row_sem,
+    input_sem, first_sem, heat_sem, pos_sem, slope_sem, tile_sem, laser_sem, back_sem, row_sem, leave_sem,
 ):
     inputs = [
         pltpu.make_async_copy(
@@ -544,6 +544,12 @@
     def put_source(i, at, block):
         ext_src[i, at : at + 8, :] = block * decay
 
+    leaving = [
+        pltpu.make_async_copy(stage.at[pl.ds(0, 384)], ref, leave_sem.at[k])
+        for k, (stage, ref) in enumerate(
+            [(position_stage, position_out), (velocity_stage, velocity_out)]
+        )
+    ]
     for turn_of in range(ROUNDS):
         out, land = tile_out.at[turn_of], tile_land.at[turn_of]
         if turn_of == 0:
@@ -570,8 +576,8 @@
                     for k in range(8):
                         ref[pl.ds(128 * c + k, 16, stride=8), :] = block[:, 16 * k : 16 * k + 16]
         if turn_of == ROUNDS - 1:
-            position_out[...] = position_stage[0:384, :]
-            velocity_out[...] = velocity_stage[0:384, :]
+            for copy in leaving:
+                copy.start()
         take(land, tile_sem.at[turn_of, 1])
         extend(lambda d: out[...] if d == (0, 0, 0) else land[WIDE.index(d)], put_level)
         for start in range(1, HALO + 1):
@@ -594,6 +600,8 @@
     take(back_out, back_sem.at[0])
     take(row_out, row_sem.at[0])
 
+    for copy in leaving:
+        copy.wait()
     take(row_land, row_sem.at[1])
     rows = row_land[:, 0, :]
     for x in range(4):
@@ -654,7 +662,7 @@
         (FOLD, 24, 128), (FOLD, 24, 128),
         (96, 128), (96, 128), (8, 1, 128), (8, 1, 128),
     ]
-    sems = [(7,), (2, 2), (2,), (STEPS, 2), (STEPS, 2), (ROUNDS, 2), (2,), (2,), (2,)]
+    sems = [(7,), (2, 2), (2,), (STEPS, 2), (STEPS, 2), (ROUNDS, 2), (2,), (2,), (2,), (2,)]
     position, velocity, level = pl.pallas_call(
         kernel,
         out_shape=(
@@ -663,7 +671,7 @@
             jax.ShapeDtypeStruct(fermion_thermal_level.shape, F32),
         ),
         in_specs=[pl.BlockSpec(memory_space=pltpu.HBM)] * 7,
-        out_specs=(vmem, vmem, vmem),
+        out_specs=(pl.BlockSpec(memory_space=pltpu.HBM),) * 2 + (vmem,),
         scratch_shapes=[pltpu.VMEM((arg.shape[0] + 8, 16), arg.dtype) for arg in args[:4]]
         + [pltpu.VMEM(arg.shape, arg.dtype) for arg in args[4:]]
         + [pltpu.VMEM((392, 16), F32)] * 2

time: 73.6 us -> 73.5 us (level)
  no operation moved by 1% of the time
where the time goes in v6:
time: 73.5 us; the launch traced here: 73.4 us
  Pallas kernels  72.7 us (99%)
    pallas_call x1, Pallas kernels, shards(): pl.pallas_call(kernel, out_shape=(jax.ShapeDtypeStruct((384, 16), F32), j...  71 us
    pallas_call x1, Pallas kernels, shards(): pl.pallas_call(deliver, out_shape=tuple((jax.ShapeDtypeStruct(result.shap...  1.75 us

profile of v6, /device:TPU:1, one launch (start us, length us, event | category | flops | bytes accessed | tf_op | source)
XLA Modules:
  0.0 73.4 jit_solution(7092760465322881996)
XLA Ops:
  0.6 71.0 %shard_map.94 = (f32[384,16]{1,0:T(8,128)}, f32[384,16]{1,0:T(8,128)}, f32[4,1,256]{2,1,0:T(1,128)}) custom-call(f32[384,16]{1,0:T(8,128)} %bitcast.8, f32[384,16]{1,0:T(8,128)} %bitcast.9, f32[768,16]{1,0:T(8,128)} %bitcast.7, s32[128,16]{1,0:T(8,128)} %bitcast.10, s32[2,4,16]{2,1,0:T(4,128)} %tally_arg.1, f32[4,1,256]{2,1,0:T(1,128)} %level_arg.1, ...), custom_call_target="tpu_custom_call" | custom-call | tf_op jit(solution)/shard_map/pallas_call | solution.py:666
  71.6 1.8 %shard_map.95 = (f32[384,16]{1,0:T(8,128)}, f32[384,16]{1,0:T(8,128)}, f32[4,1,256]{2,1,0:T(1,128)}) custom-call(f32[384,16]{1,0:T(8,128)} %get-tuple-element.9.refs_0_, f32[384,16]{1,0:T(8,128)} %get-tuple-element.10.refs_1_, f32[4,1,256]{2,1,0:T(1,128)} %get-tuple-element.11.refs_2_), custom_call_target="tpu_custom_call" | custom-call | tf_op jit(solution)/shard_map/pallas_call | solution.py:685
